TPU v7x, 512 devices: a whole 4x4x16 slice. The times are simulated.
512 devices in a mesh: crop: 8 (over x, core), dap: 64 (over y, z).
Axes of the slice: x: 4, y: 4, z: 16, core: 2. Of those that a mesh axis runs over, the one named last changes fastest.
Arguments:
- sequence_stack: bfloat16 [8, 64, 256, 256], P('crop', None, 'dap'), may hold values from -65 to 65
- upstream_derivative: bfloat16 [8, 64, 256, 256], P('crop', None, 'dap'), may hold values from -6 to 6
- coupling_logits: bfloat16 [8, 8, 256, 256], P('crop', None, 'dap'), may hold values from -6 to 300
- piece_extents: int32 [8], P('crop'), may hold values from 64 to 256, as said below
- projection_matrices: bfloat16 [4, 256, 256], replicated, may hold values from -0.375 to 0.375
- final_projection_matrix: bfloat16 [256, 256], replicated, may hold values from -0.375 to 0.375
- norm_multiplier: float32 [256], replicated, may hold values from 0.1 to 1.9
Outputs:
- sequence_stack_derivative: bfloat16 [8, 64, 256, 256], P('crop', None, 'dap')
- coupling_logit_derivative: float32 [8, 8, 256, 256], P('crop', None, 'dap')
- d_w_in: float32 [4, 256, 256], replicated
- d_w_out: float32 [256, 256], replicated
- d_gain: float32 [256], replicated
Inputs may be any that keep to these rules, and one draw needn't show every extreme that they name: `piece_extents`: in every draw one crop has 256 residues; every crop has 64 or more.
All inputs are finite; a program needn't handle non-finite values.
Results may differ from a plain program's by a relative error of at most 0.01.
Values may be sent and summed in bfloat16 or wider, within the bound.
A program may use at most 64 MiB of HBM per device.

v0:
```python
import math

import jax
import jax.numpy as jnp
from jax import lax
from jax.sharding import PartitionSpec as P

SEQUENCE_NUMBER = 64


EPSILON = 1e-05
MASKED = -1000000000.0


def product(form, left, right):
    return jnp.einsum(form, left, right, preferred_element_type=jnp.float32)


def crop_gradient_list(
    alignment_rows,
    gradient_row_list,
    head_bias,
    crop_length,
    projection_matrices,
    final_projection_matrix,
    norm_multiplier,
):
    heads = head_bias.shape[0]
    residue_count = alignment_rows.shape[1]
    channel_width = alignment_rows.shape[2]
    hidden = projection_matrices.shape[2]
    head_size = hidden // heads
    multiplier_amount = 1.0 / math.sqrt(head_size)
    valid = jnp.arange(residue_count, dtype=jnp.int32) < crop_length
    valid_rows = valid.astype(jnp.bfloat16)[:, None]
    bias_float = head_bias.astype(jnp.float32)

    def single_row(carry, input_arrays):
        bias_sum, in_sum, out_sum, gain_sum = carry
        alignment_row, gradient_row = input_arrays
        value_floats = alignment_row.astype(jnp.float32)
        centred = value_floats - jnp.mean(value_floats, axis=-1, keepdims=True)
        inv_std = lax.rsqrt(jnp.mean(centred * centred, axis=-1, keepdims=True) + EPSILON)
        normal_x = centred * inv_std
        normed = (normal_x * norm_multiplier).astype(jnp.bfloat16)
        projected = product("ic,pcd->pid", normed, projection_matrices).astype(jnp.bfloat16)
        queries = projected[0].reshape(residue_count, heads, head_size)
        keys_h = projected[1].reshape(residue_count, heads, head_size)
        vals_h = projected[2].reshape(residue_count, heads, head_size)
        scores = product("ihd,jhd->hij", queries, keys_h) * multiplier_amount + bias_float
        scores = jnp.where(valid[None, None, :], scores, MASKED)
        highest = jnp.max(scores, axis=-1, keepdims=True)
        expo = jnp.exp(scores - highest)
        probs = expo / jnp.sum(expo, axis=-1, keepdims=True)
        probs_b = probs.astype(jnp.bfloat16)
        attended = product("hij,jhd->ihd", probs_b, vals_h).reshape(residue_count, hidden)
        gate_f = jax.nn.sigmoid(projected[3].astype(jnp.float32))
        gated = (attended * gate_f).astype(jnp.bfloat16)
        masked_grad = gradient_row * valid_rows
        d_gated = product("ic,dc->id", masked_grad, final_projection_matrix)
        d_att = (d_gated * gate_f).astype(jnp.bfloat16)
        d_gate = (d_gated * attended * gate_f * (1.0 - gate_f)).astype(jnp.bfloat16)
        d_att_h = d_att.reshape(residue_count, heads, head_size)
        d_probs = product("ihd,jhd->hij", d_att_h, vals_h)
        d_vals = product("hij,ihd->jhd", probs_b, d_att_h).astype(jnp.bfloat16)
        row_total = jnp.sum(probs * d_probs, axis=-1, keepdims=True)
        d_scores = probs * (d_probs - row_total)
        d_scores_b = d_scores.astype(jnp.bfloat16)
        d_queries = (product("hij,jhd->ihd", d_scores_b, keys_h) * multiplier_amount).astype(
            jnp.bfloat16
        )
        d_keys = (product("hij,ihd->jhd", d_scores_b, queries) * multiplier_amount).astype(
            jnp.bfloat16
        )
        grads = jnp.stack(
            [
                d_queries.reshape(residue_count, hidden),
                d_keys.reshape(residue_count, hidden),
                d_vals.reshape(residue_count, hidden),
                d_gate,
            ]
        )
        d_normed = product("pid,pcd->ic", grads, projection_matrices)
        in_terms = product("ic,pid->pcd", normed, grads)
        out_term = product("id,ic->dc", gated, masked_grad)
        scaled = d_normed * norm_multiplier
        d_row = inv_std * (
            scaled
            - jnp.mean(scaled, axis=-1, keepdims=True)
            - normal_x * jnp.mean(scaled * normal_x, axis=-1, keepdims=True)
        )
        new_carry = (
            bias_sum + d_scores,
            in_sum + in_terms,
            out_sum + out_term,
            gain_sum + jnp.sum(d_normed * normal_x, axis=0),
        )
        return (new_carry, d_row.astype(jnp.bfloat16))

    crop_offset = (
        jnp.zeros(head_bias.shape, jnp.float32),
        jnp.zeros(projection_matrices.shape, jnp.float32),
        jnp.zeros(final_projection_matrix.shape, jnp.float32),
        jnp.zeros((channel_width,), jnp.float32),
    )
    gradient_totals, row_gradients = lax.scan(
        single_row, crop_offset, (alignment_rows, gradient_row_list)
    )
    return (
        row_gradients,
        gradient_totals[0],
        gradient_totals[1],
        gradient_totals[2],
        gradient_totals[3],
    )


def on_device(
    sequence_stack,
    upstream_derivative,
    coupling_logits,
    piece_extents,
    projection_matrices,
    final_projection_matrix,
    norm_multiplier,
):
    alignment_rows, gradient_row_list = (
        lax.all_to_all(sequence_stack, "dap", split_axis=1, concat_axis=2, tiled=True),
        lax.all_to_all(upstream_derivative, "dap", split_axis=1, concat_axis=2, tiled=True),
    )
    entire_bias = lax.all_gather(coupling_logits, "dap", axis=2, tiled=True)
    row_gradients, bias_part, in_part, out_part, gain_part = crop_gradient_list(
        alignment_rows[0],
        gradient_row_list[0],
        entire_bias[0],
        piece_extents[0],
        projection_matrices,
        final_projection_matrix,
        norm_multiplier,
    )
    coupling_logit_derivative = lax.psum_scatter(
        bias_part[None], "dap", scatter_dimension=2, tiled=True
    )
    sequence_stack_derivative = lax.all_to_all(
        row_gradients[None], "dap", split_axis=2, concat_axis=1, tiled=True
    )
    multiplier_amount = 1.0 / (lax.axis_size("crop") * sequence_stack.shape[0] * SEQUENCE_NUMBER)
    input_weight_sum, output_weight_sum, gate_weight_sum = lax.psum(
        (in_part, out_part, gain_part), ("crop", "dap")
    )
    return (
        sequence_stack_derivative,
        coupling_logit_derivative,
        input_weight_sum * multiplier_amount,
        output_weight_sum * multiplier_amount,
        gate_weight_sum * multiplier_amount,
    )


def solution(mesh):
    return jax.shard_map(
        on_device,
        mesh=mesh,
        in_specs=(
            P("crop", None, "dap", None),
            P("crop", None, "dap", None),
            P("crop", None, "dap", None),
            P("crop"),
            P(),
            P(),
            P(),
        ),
        out_specs=(P("crop", None, "dap", None), P("crop", None, "dap", None), P(), P(), P()),
        check_vma=False,
    )
```

profile of v0, /device:TPU:1, one launch (start us, length us, event | category | flops | bytes accessed | tf_op | source)
XLA Modules:
  0.0 1342.9 jit_solution(9764281051878207086)
XLA Ops:
  7.2 0.0 copy-start
  7.2 0.0 copy-start.7
  7.2 19.4 %all-to-all-start = ((bf16[1,64,4,256]{3,2,0,1:T(4,128)(2,1)}), bf16[1,64,4,256]{3,2,0,1:T(4,128)(2,1)S(1)}, u32[]{:S(2)}, u32[]{:S(2)}) async-start(bf16[1,64,4,256]{3,2,0,1:T(4,128)(2,1)} %bitcast.101), calls=%async_computation | async-start | bytes 262144 | tf_op jit(solution)/shard_map/all_to_all | solution.py:128
  26.6 0.0 all-gather.2.cloned.1.call-start
  26.7 1.3 copy.59
  28.0 0.0 all-gather.2.cloned.1.call-update
  28.7 0.1 copy.70
  28.8 0.5 iota_compare_fusion
  29.3 0.5 fusion.26
  29.9 10.7 all-to-all-done
  40.6 7.6 all-to-all-start.1
  48.2 0.0 all-reduce.3.cloned.1.call-start
  48.3 0.1 convert_reduce_fusion
  48.4 0.1 div.39
  48.5 0.2 multiply_reduce_fusion.3
  48.8 0.1 rsqrt.13
  48.9 13.3 all-to-all-done.1
  62.2 0.1 broadcast_multiply_fusion.2
  62.3 0.7 mul.176
  63.1 0.1 copy.56
  63.2 0.7 squeeze.30
  63.9 0.4 fusion.2
  64.3 0.8 add_divide_fusion
  65.1 0.7 fusion.29
  65.8 96.1 %all-gather.2.cloned.1.call-done = bf16[1,8,256,256]{3,1,0,2:T(8,128)(2,1)} async-done(((bf16[1,8,4,256]{3,1,0,2:T(8,128)(2,1)}), bf16[1,8,256,256]{3,1,0,2:T(8,128)(2,1)}) %all-gather.2.cloned.1.call-update) | async-done | bytes 1048592 | tf_op jit(solution)/shard_map/all_gather | solution.py:131
  161.9 2.4 copy.60
  164.3 2.2 fusion.30
  166.4 0.0 copy-start.9
  166.5 1.9 fusion.13
  168.4 0.3 fusion.14
  168.7 0.4 convolution_convert_fusion.1
  169.1 0.0 copy-done.1
  169.2 0.5 copy-done.6
  169.7 0.5 multiply_reduce_fusion
  170.2 2.0 fusion.5
  172.2 0.4 fusion.4
  172.7 0.3 fusion.3
  172.9 0.2 copy-done.3
  173.1 0.9 fusion.31
  174.0 1.4 convolution_bitcast_fusion
  175.4 0.0 all-reduce.3.cloned.1.call-update
  175.4 0.0 reduce-scatter.2.cloned.1.call-start
  175.5 2.0 copy.68
  177.5 0.0 reduce-scatter.2.cloned.1.call-update
  177.5 0.9 copy-done.11
  178.4 0.1 copy-done.13
  178.4 0.4 multiply_reduce_fusion.1
  178.8 0.1 fusion.16
  179.0 0.2 copy.67
  179.2 0.5 broadcast.134
  179.7 1.4 reduce.8
  181.1 0.7 reshape.161
  181.8 9.0 all-to-all-start.2
  190.9 114.8 %psum.23 = f32[256]{0:T(256)S(1)} all-reduce(f32[256]{0:T(256)S(1)} %get-tuple-element.67), channel_id=1, replica_groups=mesh['crop'=8,'dap'=64] {'crop','dap'}, use_global_device_ids=true, to_apply=%region_11.12 | all-reduce | flops 256 | bytes 2048 | tf_op jit(solution)/shard_map/psum | solution.py:148
  305.7 0.6 broadcast_multiply_fusion.4
  306.3 0.1 reshape.162
  306.4 0.7 bitcast_reduce_fusion
  307.1 0.7 all_to_all.11
  307.8 343.4 %all-reduce.3.cloned.1.call-done = (f32[4,256,256]{1,2,0:T(8,128)}, f32[256,256]{1,0:T(8,128)}) async-done(((f32[4,256,256]{1,2,0:T(8,128)}, f32[256,256]{1,0:T(8,128)}), (f32[4,256,256]{1,2,0:T(8,128)}, f32[256,256]{1,0:T(8,128)})) %all-reduce.3.cloned.1.call-update) | async-done | bytes 1310736 | tf_op jit(solution)/shard_map/psum | solution.py:148
  651.2 1.4 broadcast_multiply_fusion
  652.6 1.3 copy.72
  653.9 0.7 broadcast_multiply_fusion.1
  654.6 680.4 %reduce-scatter.2.cloned.1.call-done = f32[1,8,4,256]{3,1,0,2:T(8,128)} async-done(((f32[1,8,256,256]{3,1,0,2:T(8,128)}), f32[1,8,4,256]{3,1,0,2:T(8,128)}) %reduce-scatter.2.cloned.1.call-update) | async-done | bytes 32784 | tf_op jit(solution)/shard_map/reduce_scatter | solution.py:141
  1335.0 1.4 copy.71
  (28 shorter events, 0.1 us)
Async XLA Ops:
  7.2 56.7 %copy-start = (bf16[4,256,256]{2,1,0:T(8,128)(2,1)S(1)}, bf16[4,256,256]{2,1,0:T(8,128)(2,1)}, u32[]{:S(2)}) copy-start(bf16[4,256,256]{2,1,0:T(8,128)(2,1)} %param.11) | copy-start | bytes 1572868
  7.2 56.7 %copy-start.7 = (f32[256]{0:T(256)S(1)}, f32[256]{0:T(256)}, u32[]{:S(2)}) copy-start(f32[256]{0:T(256)} %param.13) | copy-start | bytes 3076
  7.2 33.4 %all-to-all-start = ((bf16[1,64,4,256]{3,2,0,1:T(4,128)(2,1)}), bf16[1,64,4,256]{3,2,0,1:T(4,128)(2,1)S(1)}, u32[]{:S(2)}, u32[]{:S(2)}) async-start(bf16[1,64,4,256]{3,2,0,1:T(4,128)(2,1)} %bitcast.101), calls=%async_computation | async-start | bytes 262144 | tf_op jit(solution)/shard_map/all_to_all | solution.py:128
  26.6 135.2 %all-gather.2.cloned.1.call-start = ((), (), s32[]{:S(2)}) async-start(), calls=%async_computation.4 | async-start | bytes 1064960 | tf_op jit(solution)/shard_map/all_gather | solution.py:131
  40.6 21.6 %all-to-all-start.1 = ((bf16[1,64,4,256]{3,2,0,1:T(4,128)(2,1)}), bf16[1,64,4,256]{3,2,0,1:T(4,128)(2,1)S(1)}, u32[]{:S(2)}, u32[]{:S(2)}) async-start(bf16[1,64,4,256]{3,2,0,1:T(4,128)(2,1)} %bitcast.102), calls=%async_computation.1 | async-start | bytes 262144 | tf_op jit(solution)/shard_map/all_to_all | solution.py:129
  48.2 603.0 %all-reduce.3.cloned.1.call-start = ((), (), s32[]{:S(2)}) async-start(), calls=%async_computation.6 | async-start | bytes 2621440 | tf_op jit(solution)/shard_map/psum | solution.py:148
  166.4 2.7 copy-start.1
  166.4 1.9 copy-start.5
  166.4 1.9 copy-start.9
  166.5 1.9 copy-start.14
  168.7 5.3 copy-start.10
  168.7 1.0 copy-start.6
  169.7 4.3 copy-start.12
  170.2 2.0 copy-start.2
  172.2 0.9 copy-start.3
  172.2 1.8 copy-start.8
  175.4 1159.6 %reduce-scatter.2.cloned.1.call-start = ((), (), s32[]{:S(2)}) async-start(), calls=%async_computation.5 | async-start | bytes 2129920 | tf_op jit(solution)/shard_map/reduce_scatter | solution.py:141
  177.5 0.9 copy-start.11
  177.5 1.0 copy-start.13
  181.8 124.4 %all-to-all-start.2 = ((bf16[64,2,512]{2,1,0:T(2,128)(2,1)}), bf16[64,2,512]{2,1,0:T(2,128)(2,1)S(1)}, u32[]{:S(2)}, u32[]{:S(2)}) async-start(bf16[64,2,512]{2,1,0:T(2,128)(2,1)} %reshape.161), calls=%async_computation.2 | async-start | bytes 262144 | tf_op jit(solution)/shard_map/all_to_all | solution.py:144
  651.2 2.7 copy-start.4
Sparse Core Ops, SparseCore 0:
  31.0 130.8 all-gather.1
  175.5 475.6 all-reduce.2
  655.6 679.3 reduce-scatter.1
where the time goes:
time: 1350 us; the launch traced here: 1340 us
  waiting for transfers between devices  1140 us (84%)
  blocking collectives  115 us (9%)
  starting transfers between devices  36.2 us (3%)
  local copies, waits for them, and re-layouts  15.7 us (1%)
  between operations  14.7 us (1%)
    reduce_scatter x1, waiting for transfers between devices, on_device(): lax.psum_scatter(bias_part[None], 'dap', scatter_dimension=2, tiled=True)  680 us
    psum x1, waiting for transfers between devices, on_device(): lax.psum((in_part, out_part, gain_part), ('crop', 'dap'))  343 us
    psum x1, blocking collectives, on_device(): lax.psum((in_part, out_part, gain_part), ('crop', 'dap'))  115 us
    all_gather x1, waiting for transfers between devices, on_device(): entire_bias = lax.all_gather(coupling_logits, 'dap', axis=2, tiled=True)  96.1 us
  transfers between devices with their start and end apart: 6, of which 5 were waited for; matrix products, arithmetic and copies ran while one was open for 1% of the time, Pallas kernels for 0%

commit v1 on v0

v1 whole, which is shorter than its diff:
```python
import functools
import math

import jax
import jax.numpy as jnp
from jax import lax
from jax.experimental import pallas as pl
from jax.experimental.pallas import tpu as pltpu
from jax.sharding import PartitionSpec as P

EPSILON = 1e-05
MASKED = -1000000000.0
LANES = 128
BF = jnp.bfloat16
F32 = jnp.float32
VMEM = pl.BlockSpec(memory_space=pltpu.VMEM)
SMEM = pl.BlockSpec(memory_space=pltpu.SMEM)
LIMIT = 28 * 1024 * 1024


class Plan:
    def __init__(self, mesh, residues, channels, heads):
        self.nc = mesh.shape["crop"]
        dap = mesh.shape["dap"]
        self.ny = 4 if dap >= 16 else 2
        self.nz = dap // self.ny
        self.qb = 4 if self.nz >= 16 else 2
        self.qa = self.nz // self.qb
        self.dap = dap
        self.n = residues
        self.c = channels
        self.heads = heads
        self.own = residues // dap
        self.msg = self.ny * self.own
        self.blk = self.nz * self.own
        self.chunks = heads // self.ny
        self.tile = self.ny * self.nz * self.own
        self.flat = 5 * channels * channels // LANES
        self.share = self.flat // self.nc
        self.quarter = self.share // self.ny
        self.extra = 16


def nn(a, b):
    return lax.dot_general(a, b, (((1,), (0,)), ((), ())), preferred_element_type=F32)


def nt(a, b):
    return lax.dot_general(a, b, (((1,), (1,)), ((), ())), preferred_element_type=F32)


def tn(a, b):
    return lax.dot_general(a, b, (((0,), (0,)), ((), ())), preferred_element_type=F32)


def swap_matrix(plan, to_z):
    size = (plan.tile, plan.tile)
    row = lax.broadcasted_iota(jnp.int32, size, 0)
    col = lax.broadcasted_iota(jnp.int32, size, 1)
    za, az = (row, col) if to_z else (col, row)
    z, a, k = za // plan.msg, (za % plan.msg) // plan.own, za % plan.own
    return jnp.where(az == a * plan.blk + z * plan.own + k, 1.0, 0.0).astype(BF)


def place(plan):
    me = lax.axis_index("dap")
    return me // plan.nz, me % plan.nz


def signal(peer):
    pl.semaphore_signal(
        pltpu.get_barrier_semaphore(), inc=1, device_id=peer, device_id_type=pl.DeviceIdType.MESH
    )


def remote(src, dst, send, recv, peer):
    return pltpu.make_async_remote_copy(
        src_ref=src,
        dst_ref=dst,
        send_sem=send,
        recv_sem=recv,
        device_id=peer,
        device_id_type=pl.DeviceIdType.MESH,
    )


def loop(count, body):
    lax.fori_loop(0, count, lambda i, c: (body(i), c)[1], 0)


def gather_kernel(
    plan, x_ref, g_ref, b_ref, xg_out, bias_out, xg_z, xg_y, b_z,
    xs, xr, gs, gr, bs, br, ys, yr, cs, cr,
):
    y, z = place(plan)
    ny, nz, blk = plan.ny, plan.nz, plan.blk

    def zpeer(i):
        zp = lax.rem(z + i + 1, nz)
        return zp, {"dap": y * nz + zp}

    def ypeer(i):
        yp = lax.rem(y + i + 1, ny)
        return yp, {"dap": yp * nz + z}

    loop(nz - 1, lambda i: signal(zpeer(i)[1]))
    loop(ny - 1, lambda i: signal(ypeer(i)[1]))
    pl.semaphore_wait(pltpu.get_barrier_semaphore(), nz + ny - 2)

    def b_copy(i):
        return remote(b_ref, b_z.at[:, z], bs.at[i], br.at[i], zpeer(i)[1])

    def x_copy(i):
        zp, peer = zpeer(i)
        return remote(x_ref.at[zp], xg_z.at[0, z], xs.at[i], xr.at[i], peer)

    def g_copy(i):
        zp, peer = zpeer(i)
        return remote(g_ref.at[zp], xg_z.at[1, z], gs.at[i], gr.at[i], peer)

    loop(nz - 1, lambda i: b_copy(i).start())
    loop(nz - 1, lambda i: x_copy(i).start())
    loop(nz - 1, lambda i: g_copy(i).start())
    b_z[:, z] = b_ref[...]
    xg_z[0, z] = x_ref[z]
    xg_z[1, z] = g_ref[z]
    swap = swap_matrix(plan, False)

    mine = pl.ds(pl.multiple_of(y * blk, blk), blk)

    def c_copy(c, i):
        part = bias_out.at[pl.ds(c * ny, ny), mine]
        return remote(part, part, cs.at[c, i], cr.at[c, i], ypeer(i)[1])

    loop(nz - 1, lambda i: b_copy(i).wait_recv())
    for c in range(plan.chunks):
        rows = nn(swap, b_z[c].reshape(plan.tile, plan.n)).astype(BF)
        bias_out[pl.ds(c * ny, ny), mine] = rows.reshape(ny, blk, plan.n)
        for i in range(ny - 1):
            c_copy(c, i).start()

    def y_copy(i):
        yp, peer = ypeer(i)
        return remote(xg_y.at[:, yp], xg_out.at[:, y], ys.at[i], yr.at[i], peer)

    loop(nz - 1, lambda i: x_copy(i).wait_recv())
    loop(nz - 1, lambda i: g_copy(i).wait_recv())
    for t in range(2):
        rows = nn(swap, xg_z[t].reshape(plan.tile, plan.c)).astype(BF)
        xg_y[t] = rows.reshape(ny, blk, plan.c)
    for i in range(ny - 1):
        y_copy(i).start()
    xg_out[:, y] = xg_y[:, y]

    for i in range(ny - 1):
        y_copy(i).wait_recv()
    for c in range(plan.chunks):
        for i in range(ny - 1):
            c_copy(c, i).wait_recv()
            c_copy(c, i).wait_send()
    for i in range(ny - 1):
        y_copy(i).wait_send()
    loop(nz - 1, lambda i: b_copy(i).wait_send())
    loop(nz - 1, lambda i: x_copy(i).wait_send())
    loop(nz - 1, lambda i: g_copy(i).wait_send())


def compute_kernel(
    plan, ext_ref, xg_ref, bias_ref, win_ref, wout_ref, gain_ref, dr_ref, ds_ref, wg_ref
):
    n, ch = plan.n, plan.c
    size = ch // plan.heads
    mult = 1.0 / math.sqrt(size)
    extent = ext_ref[0]
    gain = gain_ref[...]
    value = xg_ref[0].astype(F32)
    centred = value - jnp.mean(value, axis=-1, keepdims=True)
    inv_std = lax.rsqrt(jnp.mean(centred * centred, axis=-1, keepdims=True) + EPSILON)
    normal = centred * inv_std
    normed = (normal * gain).astype(BF)
    q, k, v, gl = [nn(normed, win_ref[p]).astype(BF) for p in range(4)]
    gate = jax.nn.sigmoid(gl.astype(F32))
    row_valid = lax.broadcasted_iota(jnp.int32, (n, ch), 0) < extent
    mg = jnp.where(row_valid, xg_ref[1].astype(F32), 0.0).astype(BF)
    d_gated = nt(mg, wout_ref[...])
    da = (d_gated * gate).astype(BF)
    col_valid = lax.broadcasted_iota(jnp.int32, (n, n), 1) < extent
    head_of = lax.broadcasted_iota(jnp.int32, (1, ch), 1) // size
    att = dv = dq = dk = jnp.zeros((n, ch), F32)
    for h in range(plan.heads):
        own = jnp.where(head_of == h, 1.0, 0.0).astype(BF)
        qh, kh, vh, dah = q * own, k * own, v * own, da * own
        scores = nt(qh, k) * mult + bias_ref[h].astype(F32)
        scores = jnp.where(col_valid, scores, MASKED)
        expo = jnp.exp(scores - jnp.max(scores, axis=-1, keepdims=True))
        probs = expo * (1.0 / jnp.sum(expo, axis=-1, keepdims=True))
        pb = probs.astype(BF)
        d_probs = nt(dah, v)
        total = jnp.sum(probs * d_probs, axis=-1, keepdims=True)
        dsb = (probs * (d_probs - total)).astype(BF)
        ds_ref[h] = dsb
        att += nn(pb, vh)
        dv += tn(pb, dah)
        dq += nn(dsb, kh)
        dk += tn(dsb, qh)
    gated = (att * gate).astype(BF)
    grads = [
        (dq * mult).astype(BF),
        (dk * mult).astype(BF),
        dv.astype(BF),
        (d_gated * att * gate * (1.0 - gate)).astype(BF),
    ]
    d_normed = jnp.zeros((n, ch), F32)
    for p in range(4):
        d_normed += nt(grads[p], win_ref[p])
    scaled = d_normed * gain
    d_row = inv_std * (
        scaled
        - jnp.mean(scaled, axis=-1, keepdims=True)
        - normal * jnp.mean(scaled * normal, axis=-1, keepdims=True)
    )
    dr_ref[...] = d_row.astype(BF)

    share = plan.share

    def keep(start, part):
        at = start
        while at < start + ch:
            c = at // share
            end = min(start + ch, (c + 1) * share)
            wg_ref[c, at - c * share : end - c * share] = part[at - start : end - start]
            at = end

    for t in range(5):
        term = tn(normed, grads[t]) if t < 4 else tn(gated, mg)
        for half in range(2):
            part = term[:, half * LANES : (half + 1) * LANES].astype(BF)
            keep((2 * t + half) * ch, part)
    d_gain = jnp.sum(d_normed * normal, axis=0, keepdims=True)
    line = lax.broadcasted_iota(jnp.int32, (plan.extra, LANES), 0)
    lo = jnp.broadcast_to(d_gain[:, :LANES], (plan.extra, LANES))
    hi = jnp.broadcast_to(d_gain[:, LANES:], (plan.extra, LANES))
    block = jnp.where(line == 0, lo, jnp.where(line == 1, hi, 0.0)).astype(BF)
    for c in range(plan.nc):
        wg_ref[c, share : share + plan.extra] = block


def scatter_kernel(
    plan, dr_ref, ds_ref, wg_ref, dr_out, db_out, w_out, gain_out,
    dr_y, dr_z, ds_y, ds_z, ds_in, w_c, w_y, w_yin, w_a, w_b, w_q, w_s,
    dys, dyr, dzs, dzr, sys_, syr, szs, szr, wcs, wcr, wys, wyr, was, war, wbs, wbr,
    gys, gyr, gcs, gcr,
):
    y, z = place(plan)
    crop = lax.axis_index("crop")
    ny, nz, nc, blk, qa, qb = plan.ny, plan.nz, plan.nc, plan.blk, plan.qa, plan.qb
    za, zb = z // qb, z % qb
    share, quarter = plan.share, plan.quarter

    def zpeer(i):
        zp = lax.rem(z + i + 1, nz)
        return zp, {"dap": y * nz + zp}

    def ypeer(i):
        yp = lax.rem(y + i + 1, ny)
        return yp, {"dap": yp * nz + z}

    def cpeer(i):
        cp = lax.rem(crop + i + 1, nc)
        return cp, {"crop": cp}

    loop(nz - 1, lambda i: signal(zpeer(i)[1]))
    loop(ny - 1, lambda i: signal(ypeer(i)[1]))
    loop(nc - 1, lambda i: signal(cpeer(i)[1]))
    pl.semaphore_wait(pltpu.get_barrier_semaphore(), nz + ny + nc - 3)

    def dr_ycopy(i):
        yp, peer = ypeer(i)
        return remote(dr_ref.at[yp], dr_y.at[y], dys.at[i], dyr.at[i], peer)

    def dr_zcopy(i):
        zp, peer = zpeer(i)
        return remote(dr_z.at[zp], dr_out.at[z], dzs.at[i], dzr.at[i], peer)

    def ds_ycopy(c, i):
        yp, peer = ypeer(i)
        part = ds_ref.at[pl.ds(c * ny, ny), yp]
        return remote(part, ds_y.at[c, i], sys_.at[c, i], syr.at[c, i], peer)

    def ds_zcopy(c, i):
        zp, peer = zpeer(i)
        return remote(ds_z.at[c, zp], ds_in.at[c, z], szs.at[c, i], szr.at[c, i], peer)

    def w_ccopy(i):
        cp, peer = cpeer(i)
        return remote(wg_ref.at[cp], w_c.at[crop], wcs.at[i], wcr.at[i], peer)

    def w_ycopy(i):
        yp, peer = ypeer(i)
        return remote(w_y.at[yp], w_yin.at[y], wys.at[i], wyr.at[i], peer)

    def w_acopy(i):
        peer = {"dap": y * nz + za * qb + lax.rem(zb + i + 1, qb)}
        return remote(w_a.at[zb], w_a.at[zb], was.at[i], war.at[i], peer)

    def w_bcopy(i):
        peer = {"dap": y * nz + lax.rem(za + i + 1, qa) * qb + zb}
        return remote(w_b.at[za], w_b.at[za], wbs.at[i], wbr.at[i], peer)

    def g_ycopy(i):
        part = w_q.at[y]
        return remote(part, part, gys.at[i], gyr.at[i], ypeer(i)[1])

    def g_ccopy(i):
        part = w_out.at[crop]
        return remote(w_s, part, gcs.at[i], gcr.at[i], cpeer(i)[1])

    for i in range(ny - 1):
        dr_ycopy(i).start()
    loop(nc - 1, lambda i: w_ccopy(i).start())
    for c in range(plan.chunks):
        for i in range(ny - 1):
            ds_ycopy(c, i).start()
    dr_y[y] = dr_ref[y]
    w_c[crop] = wg_ref[crop]
    swap = swap_matrix(plan, True)

    for i in range(ny - 1):
        dr_ycopy(i).wait_recv()
    rows = nn(swap, dr_y[...].reshape(plan.tile, plan.c)).astype(BF)
    dr_z[...] = rows.reshape(nz, plan.msg, plan.c)
    loop(nz - 1, lambda i: dr_zcopy(i).start())
    dr_out[z] = dr_z[z]

    def fold(c):
        for i in range(ny - 1):
            ds_ycopy(c, i).wait_recv()
        total = ds_ref[pl.ds(c * ny, ny), y].astype(F32)
        for i in range(ny - 1):
            total += ds_y[c, i].astype(F32)
        rows = nn(swap, total.astype(BF).reshape(plan.tile, plan.n)).astype(BF)
        ds_z[c] = rows.reshape(nz, plan.msg, plan.n)
        loop(nz - 1, lambda i: ds_zcopy(c, i).start())
        ds_in[c, z] = ds_z[c, z]

    half = (plan.chunks + 1) // 2
    for c in range(half):
        fold(c)

    loop(nc - 1, lambda i: w_ccopy(i).wait_recv())
    total = w_c[0].astype(F32)
    for i in range(1, nc):
        total += w_c[i].astype(F32)
    total = total.astype(BF)
    for i in range(ny):
        w_y[i, :quarter] = total[i * quarter : (i + 1) * quarter]
        w_y[i, quarter:] = total[share:]
    for i in range(ny - 1):
        w_ycopy(i).start()
    w_yin[y] = w_y[y]

    for c in range(half, plan.chunks):
        fold(c)

    def summed(ref, count):
        out = ref[0].astype(F32)
        for i in range(1, count):
            out += ref[i].astype(F32)
        return out

    for i in range(ny - 1):
        w_ycopy(i).wait_recv()
    w_a[zb] = summed(w_yin, ny).astype(BF)
    for i in range(qb - 1):
        w_acopy(i).start()
    for i in range(qb - 1):
        w_acopy(i).wait_recv()
    w_b[za] = summed(w_a, qb).astype(BF)
    for i in range(qa - 1):
        w_bcopy(i).start()
    for i in range(qa - 1):
        w_bcopy(i).wait_recv()
    total = summed(w_b, qa)
    gain_out[...] = total[quarter:]
    w_q[y] = total[:quarter].astype(BF)
    for i in range(ny - 1):
        g_ycopy(i).start()
    for i in range(ny - 1):
        g_ycopy(i).wait_recv()
    for i in range(ny):
        w_s[pl.ds(i * quarter, quarter)] = w_q[i]
    loop(nc - 1, lambda i: g_ccopy(i).start())
    w_out[crop] = w_s[...]

    for c in range(plan.chunks):
        loop(nz - 1, lambda i: ds_zcopy(c, i).wait_recv())
        db_out[c] = summed(ds_in.at[c], nz)
    loop(nz - 1, lambda i: dr_zcopy(i).wait_recv())
    loop(nc - 1, lambda i: g_ccopy(i).wait_recv())

    for i in range(ny - 1):
        dr_ycopy(i).wait_send()
        w_ycopy(i).wait_send()
        g_ycopy(i).wait_send()
        for c in range(plan.chunks):
            ds_ycopy(c, i).wait_send()
    for i in range(qb - 1):
        w_acopy(i).wait_send()
    for i in range(qa - 1):
        w_bcopy(i).wait_send()
    loop(nc - 1, lambda i: w_ccopy(i).wait_send())
    loop(nc - 1, lambda i: g_ccopy(i).wait_send())
    loop(nz - 1, lambda i: dr_zcopy(i).wait_send())
    for c in range(plan.chunks):
        loop(nz - 1, lambda i: ds_zcopy(c, i).wait_send())


def dma(*shape):
    return pltpu.SemaphoreType.DMA(shape)


def on_device(plan, x, upstream, bias, extents, w_in, w_final, gain):
    ny, nz, nc, n, ch = plan.ny, plan.nz, plan.nc, plan.n, plan.c
    msg, blk, chunks = plan.msg, plan.blk, plan.chunks
    xg, full = pl.pallas_call(
        functools.partial(gather_kernel, plan),
        out_shape=(
            jax.ShapeDtypeStruct((2, ny, blk, ch), BF),
            jax.ShapeDtypeStruct((plan.heads, n, n), BF),
        ),
        in_specs=[VMEM] * 3,
        out_specs=(VMEM, VMEM),
        scratch_shapes=[
            pltpu.VMEM((2, nz, msg, ch), BF),
            pltpu.VMEM((2, ny, blk, ch), BF),
            pltpu.VMEM((chunks, nz, msg, n), BF),
            *[dma(nz - 1)] * 6,
            *[dma(ny - 1)] * 2,
            *[dma(chunks, ny - 1)] * 2,
        ],
        compiler_params=pltpu.CompilerParams(
            collective_id=0, has_side_effects=True, vmem_limit_bytes=LIMIT
        ),
        name="gather_rows",
    )(
        x.reshape(nz, msg, ch),
        upstream.reshape(nz, msg, ch),
        bias.reshape(chunks, msg, n),
    )
    total = plan.share + plan.extra
    dr, ds, wg = pl.pallas_call(
        functools.partial(compute_kernel, plan),
        out_shape=(
            jax.ShapeDtypeStruct((n, ch), BF),
            jax.ShapeDtypeStruct((plan.heads, n, n), BF),
            jax.ShapeDtypeStruct((nc, total, LANES), BF),
        ),
        in_specs=[SMEM] + [VMEM] * 5,
        out_specs=(VMEM, VMEM, VMEM),
        compiler_params=pltpu.CompilerParams(vmem_limit_bytes=LIMIT),
        name="row_gradients",
    )(extents, xg.reshape(2, n, ch), full, w_in, w_final, gain.reshape(1, ch))
    part = plan.quarter + plan.extra
    d_rows, d_bias, w_sum, gain_sum = pl.pallas_call(
        functools.partial(scatter_kernel, plan),
        out_shape=(
            jax.ShapeDtypeStruct((nz, msg, ch), BF),
            jax.ShapeDtypeStruct((chunks, msg, n), F32),
            jax.ShapeDtypeStruct((nc, plan.share, LANES), BF),
            jax.ShapeDtypeStruct((plan.extra, LANES), F32),
        ),
        in_specs=[VMEM] * 3,
        out_specs=(VMEM,) * 4,
        scratch_shapes=[
            pltpu.VMEM((ny, blk, ch), BF),
            pltpu.VMEM((nz, msg, ch), BF),
            pltpu.VMEM((chunks, ny - 1, ny, blk, n), BF),
            pltpu.VMEM((chunks, nz, msg, n), BF),
            pltpu.VMEM((chunks, nz, msg, n), BF),
            pltpu.VMEM((nc, total, LANES), BF),
            pltpu.VMEM((ny, part, LANES), BF),
            pltpu.VMEM((ny, part, LANES), BF),
            pltpu.VMEM((plan.qb, part, LANES), BF),
            pltpu.VMEM((plan.qa, part, LANES), BF),
            pltpu.VMEM((ny, plan.quarter, LANES), BF),
            pltpu.VMEM((plan.share, LANES), BF),
            *[dma(ny - 1)] * 2,
            *[dma(nz - 1)] * 2,
            *[dma(chunks, ny - 1)] * 2,
            *[dma(chunks, nz - 1)] * 2,
            *[dma(nc - 1)] * 2,
            *[dma(ny - 1)] * 2,
            *[dma(plan.qb - 1)] * 2,
            *[dma(plan.qa - 1)] * 2,
            *[dma(ny - 1)] * 2,
            *[dma(nc - 1)] * 2,
        ],
        compiler_params=pltpu.CompilerParams(
            collective_id=1, has_side_effects=True, vmem_limit_bytes=LIMIT
        ),
        name="scatter_gradients",
    )(
        dr.reshape(ny, blk, ch),
        ds.reshape(plan.heads, ny, blk, n),
        wg,
    )
    scale = 1.0 / (nc * plan.dap)
    w_sum = w_sum.reshape(5, 2, ch, LANES).transpose(0, 2, 1, 3).reshape(5, ch, ch)
    w_sum = w_sum.astype(F32) * scale
    return (
        d_rows.reshape(x.shape),
        d_bias.reshape(bias.shape),
        w_sum[:4],
        w_sum[4],
        gain_sum[:2].reshape(ch) * scale,
    )


def solution(mesh):
    split = P("crop", None, "dap", None)

    def whole(*arrays):
        plan = Plan(mesh, arrays[0].shape[2], arrays[0].shape[3], arrays[2].shape[1])
        return jax.shard_map(
            functools.partial(on_device, plan),
            mesh=mesh,
            in_specs=(split, split, split, P("crop"), P(), P(), P()),
            out_specs=(split, split, P(), P(), P()),
            check_vma=False,
        )(*arrays)

    return whole
```

time: 1350 us -> 116 us (0.09)
  waiting for transfers between devices: 1140 us -> 0 us
  blocking collectives: 115 us -> 0 us
  Pallas kernels: 0 us -> 105 us
  starting transfers between devices: 36.2 us -> 0 us
    reduce_scatter x1 -> x0, waiting for transfers between devices: 680 us -> none  [on_device(): lax.psum_scatter(bias_part[None], 'dap', scatter_dimension=2, tiled=True)]
    psum x1 -> x0, waiting for transfers between devices: 343 us -> none  [on_device(): lax.psum((in_part, out_part, gain_part), ('crop', 'dap'))]
    psum x1 -> x0, blocking collectives: 115 us -> none  [on_device(): lax.psum((in_part, out_part, gain_part), ('crop', 'dap'))]
    pallas_call x0 -> x3, Pallas kernels: none -> 105 us  [the longest x1 55.5 us: on_device(): pl.pallas_call(functools.partial(scatter_kernel, plan), out_shape=(jax.Sh...]
    all_gather x1 -> x0, waiting for transfers between devices: 96.1 us -> none  [on_device(): entire_bias = lax.all_gather(coupling_logits, 'dap', axis=2, tiled=True)]
    all_to_all x3 -> x0, starting transfers between devices: 36.1 us -> none  [the longest x1 19.4 us: on_device(): lax.all_to_all(sequence_stack, 'dap', split_axis=1, concat_axis=2, tiled=...]
    all_to_all x3 -> x0, waiting for transfers between devices: 24 us -> none  [the longest x1 13.3 us: on_device(): lax.all_to_all(upstream_derivative, 'dap', split_axis=1, concat_axis=2, t...]
  transfers between devices with their start and end apart: 6 -> 0, of which waited for: 5 -> 0; matrix products, arithmetic and copies ran while one was open for 1% -> 0% of each run, Pallas kernels for 0% -> 0%
where the time goes in v1:
time: 116 us
  Pallas kernels  105 us (91%)
  local copies, waits for them, and re-layouts  8.55 us (7%)
  between operations  1.33 us (1%)
    pallas_call x1, Pallas kernels, on_device(): pl.pallas_call(functools.partial(scatter_kernel, plan), out_shape=(jax.Sh...  55.5 us
    pallas_call x1, Pallas kernels, on_device(): pl.pallas_call(functools.partial(gather_kernel, plan), out_shape=(jax.Sha...  44.8 us
    pallas_call x1, Pallas kernels, on_device(): pl.pallas_call(functools.partial(compute_kernel, plan), out_shape=(jax.Sh...  4.75 us
    unnamed x7, local copies, waits for them, and re-layouts  3.34 us

profile of v1, /device:TPU:1, one launch (start us, length us, event | category | flops | bytes accessed | tf_op | source)
XLA Modules:
  0.0 115.5 jit_solution(17497764615367182863)
XLA Ops:
  1.3 0.7 reshape.53.b_ref
  2.0 0.9 reshape.51.x_ref
  2.9 0.9 reshape.52.g_ref
  3.9 44.8 %gather_rows.1 = (bf16[2,4,64,256]{3,2,1,0:T(8,128)(2,1)S(1)}, bf16[8,256,256]{2,1,0:T(8,128)(2,1)S(1)}) custom-call(bf16[16,16,256]{2,1,0:T(8,128)(2,1)S(1)} %reshape.51.x_ref, bf16[16,16,256]{2,1,0:T(8,128)(2,1)S(1)} %reshape.52.g_ref, bf16[2,16,256]{2,1,0:T(8,128)(2,1)S(1)} %reshape.53.b_ref), custom_call_target="tpu_custom_call" | custom-call | tf_op jit(solution)/shard_map/gather_rows/pallas_call | solution.py:425
  48.7 0.0 copy-start
  48.7 1.0 copy-done
  49.7 0.0 copy-start.1
  49.7 0.9 copy-done.1
  50.6 0.0 copy-start.2
  50.6 0.7 copy-done.2
  51.3 4.8 %row_gradients.1 = (bf16[256,256]{1,0:T(8,128)(2,1)S(1)}, bf16[8,256,256]{2,1,0:T(8,128)(2,1)S(1)}, bf16[8,336,128]{2,1,0:T(8,128)(2,1)S(1)}) custom-call(s32[1]{0:T(128)S(6)} %copy.19.ext_ref, bf16[2,256,256]{2,1,0:T(8,128)(2,1)S(1)} %bitcast.20, bf16[8,256,256]{2,1,0:T(8,128)(2,1)S(1)} %get-tuple-element.15.bias_ref, bf16[4,256,256]{2,1,0:T(8,128)(2,1)S(1)} %copy-done, ...), custom_call_target="tpu_custom_call" | custom-call | tf_op jit(solution)/shard_map/row_gradients/pallas_call | solution.py:451
  56.1 55.5 %scatter_gradients.1 = (bf16[16,16,256]{2,1,0:T(8,128)(2,1)S(1)}, f32[2,16,256]{2,1,0:T(8,128)S(1)}, bf16[8,320,128]{2,1,0:T(8,128)(2,1)S(1)}, f32[16,128]{1,0:T(8,128)S(1)}) custom-call(bf16[4,64,256]{2,1,0:T(8,128)(2,1)S(1)} %bitcast.21, bf16[8,4,64,256]{3,2,1,0:T(8,128)(2,1)S(1)} %bitcast.19, bf16[8,336,128]{2,1,0:T(8,128)(2,1)S(1)} %get-tuple-element.18.wg_ref), custom_call_target="tpu_custom_call" | custom-call | tf_op jit(solution)/shard_map/scatter_gradients/pallas_call | solution.py:464
  111.6 0.7 reshape.58
  112.2 0.6 multiply_bitcast_fusion
  112.8 0.6 reshape.59
  113.4 0.1 convert_multiply_fusion
  113.6 1.1 copy_bitcast_fusion
  114.6 0.2 copy.13
  114.8 0.7 copy.18
  (1 shorter events, 0.0 us)
Async XLA Ops:
  48.7 1.0 copy-start
  49.7 0.9 copy-start.1
  50.6 0.7 copy-start.2

commit v2 on v1

v2 whole, which is shorter than its diff:
```python
import functools
import math

import jax
import jax.numpy as jnp
from jax import lax
from jax.experimental import pallas as pl
from jax.experimental.pallas import tpu as pltpu
from jax.sharding import PartitionSpec as P

EPSILON = 1e-05
MASKED = -1000000000.0
LANES = 128
BF = jnp.bfloat16
F32 = jnp.float32
ANY = pl.BlockSpec(memory_space=pl.ANY)
VMEM = pl.BlockSpec(memory_space=pltpu.VMEM)
SMEM = pl.BlockSpec(memory_space=pltpu.SMEM)
LIMIT = 44 * 1024 * 1024


class Plan:
    def __init__(self, mesh, residues, channels, heads):
        self.nc = mesh.shape["crop"]
        self.nx = self.nc // 2
        dap = mesh.shape["dap"]
        self.ny = 4 if dap >= 16 else 2
        self.nz = dap // self.ny
        self.qb = 4 if self.nz >= 16 else 2
        self.qa = self.nz // self.qb
        self.dap = dap
        self.n = residues
        self.c = channels
        self.heads = heads
        self.own = residues // dap
        self.msg = self.ny * self.own
        self.blk = self.nz * self.own
        self.chunks = heads // self.ny
        self.tile = self.ny * self.nz * self.own
        self.flat = 5 * channels * channels // LANES
        self.share = self.flat // self.nc
        self.quarter = self.share // self.ny
        self.extra = 16


def nn(a, b):
    return lax.dot_general(a, b, (((1,), (0,)), ((), ())), preferred_element_type=F32)


def nt(a, b):
    return lax.dot_general(a, b, (((1,), (1,)), ((), ())), preferred_element_type=F32)


def tn(a, b):
    return lax.dot_general(a, b, (((0,), (0,)), ((), ())), preferred_element_type=F32)


def swap_matrix(plan, to_z):
    size = (plan.tile, plan.tile)
    row = lax.broadcasted_iota(jnp.int32, size, 0)
    col = lax.broadcasted_iota(jnp.int32, size, 1)
    za, az = (row, col) if to_z else (col, row)
    z, a, k = za // plan.msg, (za % plan.msg) // plan.own, za % plan.own
    return jnp.where(az == a * plan.blk + z * plan.own + k, 1.0, 0.0).astype(BF)


def place(plan):
    me = lax.axis_index("dap")
    return me // plan.nz, me % plan.nz


def signal(peer):
    pl.semaphore_signal(
        pltpu.get_barrier_semaphore(), inc=1, device_id=peer, device_id_type=pl.DeviceIdType.MESH
    )


def remote(src, dst, send, recv, peer):
    return pltpu.make_async_remote_copy(
        src_ref=src,
        dst_ref=dst,
        send_sem=send,
        recv_sem=recv,
        device_id=peer,
        device_id_type=pl.DeviceIdType.MESH,
    )


def loop(count, body):
    lax.fori_loop(0, count, lambda i, c: (body(i), c)[1], 0)


def keep(plan, put):
    for t in range(5):
        for half in range(2):
            start = (2 * t + half) * plan.c
            at = start
            while at < start + plan.c:
                s = at // plan.share
                end = min(start + plan.c, (s + 1) * plan.share)
                low = s * plan.share
                put(t, half, slice(at - start, end - start), s, slice(at - low, end - low))
                at = end


def summed(ref, count):
    out = ref[0].astype(F32)
    for i in range(1, count):
        out += ref[i].astype(F32)
    return out


def whole_kernel(
    plan, ext_ref, x_hbm, g_hbm, b_hbm, win_hbm, wout_hbm, gain_hbm,
    dr_out, db_out, win_out, wout_out, gain_out,
    x_in, g_in, b_in, win_ref, wout_ref, gain_ref,
    xg_s, xg_y, xg_zs, xg_z, b_z, bias_ref, ds_ref, ds_y, ds_zs, ds_z,
    dr_s, dr_y, dr_zs, dr_z, wg, w_cin, w_x, w_xin, w_y, w_yin, w_a, w_b, w_all,
    lsem, xy, xz, bf, bn, by, dy, dz, ry, rz, wc, wx, wy, wa, wb, gy, gx, gc,
):
    y, z = place(plan)
    crop = lax.axis_index("crop")
    cx, core = crop // 2, crop % 2
    ny, nz, nx, blk, qa, qb = plan.ny, plan.nz, plan.nx, plan.blk, plan.qa, plan.qb
    za, zb = z // qb, z % qb
    n, ch, msg = plan.n, plan.c, plan.msg
    share, quarter, extra = plan.share, plan.quarter, plan.extra

    def zpeer(i):
        step = (i + 1) // 2
        zp = lax.rem(z + nz // 2 + step * (1 - 2 * (i % 2)), nz)
        return zp, {"dap": y * nz + zp}

    def ypeer(i):
        yp = lax.rem(y + i + 1, ny)
        return yp, {"dap": yp * nz + z}

    def xpeer(i):
        xp = lax.rem(cx + i + 1, nx)
        return xp, {"crop": xp * 2 + core}

    def apeer(i):
        return {"dap": y * nz + lax.rem(za + i + 1, qa) * qb + zb}

    def bpeer(i):
        return {"dap": y * nz + za * qb + lax.rem(zb + i + 1, qb)}

    other = {"crop": cx * 2 + 1 - core}

    local = [
        pltpu.make_async_copy(s, d, lsem.at[i])
        for i, (s, d) in enumerate(
            [
                (b_hbm, b_in), (x_hbm, x_in), (g_hbm, g_in),
                (win_hbm, win_ref), (wout_hbm, wout_ref), (gain_hbm, gain_ref),
            ]
        )
    ]
    for c in local:
        c.start()
    loop(nz - 1, lambda i: signal(zpeer(i)[1]))
    for i in range(ny - 1):
        signal(ypeer(i)[1])
    for i in range(nx - 1):
        signal(xpeer(i)[1])
    signal(other)
    for c in local[:3]:
        c.wait()
    b_z[:, za, zb] = b_in[...].reshape(plan.chunks, msg, n)
    xg_s[0] = x_in[...].reshape(ny, blk, ch)
    xg_s[1] = g_in[...].reshape(ny, blk, ch)
    to_y = swap_matrix(plan, False)
    to_z = swap_matrix(plan, True)
    pl.semaphore_wait(pltpu.get_barrier_semaphore(), nz + ny + nx - 2)

    def b_far(i):
        part = b_z.at[:, za, zb]
        return remote(part, part, bf.at[0, i], bf.at[1, i], apeer(i))

    def b_near(i):
        part = b_z.at[:, :, zb]
        return remote(part, part, bn.at[0, i], bn.at[1, i], bpeer(i))

    mine = pl.ds(pl.multiple_of(y * blk, blk), blk)

    def b_y(c, i):
        part = bias_ref.at[pl.ds(c * ny, ny), mine]
        return remote(part, part, by.at[0, c, i], by.at[1, c, i], ypeer(i)[1])

    def x_y(i):
        yp, peer = ypeer(i)
        return remote(xg_s.at[:, yp], xg_y.at[:, y], xy.at[0, i], xy.at[1, i], peer)

    def x_z(i):
        zp, peer = zpeer(i)
        return remote(xg_zs.at[:, zp], xg_z.at[:, z], xz.at[0, i], xz.at[1, i], peer)

    for i in range(qa - 1):
        b_far(i).start()
    for i in range(ny - 1):
        x_y(i).start()
    xg_y[:, y] = xg_s[:, y]
    for i in range(qa - 1):
        b_far(i).wait_recv()
    for i in range(qb - 1):
        b_near(i).start()
    for i in range(ny - 1):
        x_y(i).wait_recv()
    for t in range(2):
        rows = nn(to_z, xg_y[t].reshape(plan.tile, ch)).astype(BF)
        xg_zs[t] = rows.reshape(nz, msg, ch)
    loop(nz - 1, lambda i: x_z(i).start())
    xg_z[:, z] = xg_zs[:, z]
    for i in range(qb - 1):
        b_near(i).wait_recv()
    for c in range(plan.chunks):
        rows = nn(to_y, b_z[c].reshape(plan.tile, n)).astype(BF)
        bias_ref[pl.ds(c * ny, ny), mine] = rows.reshape(ny, blk, n)
        for i in range(ny - 1):
            b_y(c, i).start()
    for c in local[3:]:
        c.wait()
    loop(nz - 1, lambda i: x_z(i).wait_recv())

    size = ch // plan.heads
    mult = 1.0 / math.sqrt(size)
    extent = ext_ref[0]
    gain = gain_ref[...]
    value = nn(to_y, xg_z[0].reshape(plan.tile, ch))
    upstream = nn(to_y, xg_z[1].reshape(plan.tile, ch))
    centred = value - jnp.mean(value, axis=-1, keepdims=True)
    inv_std = lax.rsqrt(jnp.mean(centred * centred, axis=-1, keepdims=True) + EPSILON)
    normal = centred * inv_std
    normed = (normal * gain).astype(BF)
    q, k, v, gl = [nn(normed, win_ref[p]).astype(BF) for p in range(4)]
    gate = jax.nn.sigmoid(gl.astype(F32))
    row_valid = lax.broadcasted_iota(jnp.int32, (n, ch), 0) < extent
    mg = jnp.where(row_valid, upstream, 0.0).astype(BF)
    d_gated = nt(mg, wout_ref[...])
    da = (d_gated * gate).astype(BF)
    col_valid = lax.broadcasted_iota(jnp.int32, (n, n), 1) < extent
    head_of = lax.broadcasted_iota(jnp.int32, (1, ch), 1) // size
    att = dv = dq = dk = jnp.zeros((n, ch), F32)

    def ds_ycopy(c, i):
        yp, peer = ypeer(i)
        part = ds_ref.at[pl.ds(c * ny, ny), yp]
        return remote(part, ds_y.at[c, i], dy.at[0, c, i], dy.at[1, c, i], peer)

    for h in range(plan.heads):
        if h % ny == 0:
            for i in range(ny - 1):
                b_y(h // ny, i).wait_recv()
        own = jnp.where(head_of == h, 1.0, 0.0).astype(BF)
        qh, kh, vh, dah = q * own, k * own, v * own, da * own
        scores = nt(qh, k) * mult + bias_ref[h].astype(F32)
        scores = jnp.where(col_valid, scores, MASKED)
        expo = jnp.exp(scores - jnp.max(scores, axis=-1, keepdims=True))
        probs = expo * (1.0 / jnp.sum(expo, axis=-1, keepdims=True))
        pb = probs.astype(BF)
        d_probs = nt(dah, v)
        total = jnp.sum(probs * d_probs, axis=-1, keepdims=True)
        dsb = (probs * (d_probs - total)).astype(BF)
        ds_ref[h] = dsb.reshape(ny, blk, n)
        att += nn(pb, vh)
        dv += tn(pb, dah)
        dq += nn(dsb, kh)
        dk += tn(dsb, qh)
        if h % ny == ny - 1:
            for i in range(ny - 1):
                ds_ycopy(h // ny, i).start()
    gated = (att * gate).astype(BF)
    grads = [
        (dq * mult).astype(BF),
        (dk * mult).astype(BF),
        dv.astype(BF),
        (d_gated * att * gate * (1.0 - gate)).astype(BF),
    ]
    d_normed = jnp.zeros((n, ch), F32)
    for p in range(4):
        d_normed += nt(grads[p], win_ref[p])
    terms = [tn(normed, grads[p]).astype(BF) for p in range(4)] + [tn(gated, mg).astype(BF)]

    def put(t, half, rows, s, at):
        wg[s // nx, s % nx, at] = terms[t][rows, half * LANES : (half + 1) * LANES]

    keep(plan, put)
    d_gain = jnp.sum(d_normed * normal, axis=0, keepdims=True)
    line = lax.broadcasted_iota(jnp.int32, (extra, LANES), 0)
    lo = jnp.broadcast_to(d_gain[:, :LANES], (extra, LANES))
    hi = jnp.broadcast_to(d_gain[:, LANES:], (extra, LANES))
    block = jnp.where(line == 0, lo, jnp.where(line == 1, hi, 0.0)).astype(BF)
    for c in range(plan.nc):
        wg[c // nx, c % nx, share:] = block

    def w_core():
        return remote(wg.at[1 - core], w_cin, wc.at[0], wc.at[1], other)

    def w_xcopy(i):
        xp, peer = xpeer(i)
        return remote(w_x.at[xp], w_xin.at[cx], wx.at[0, i], wx.at[1, i], peer)

    def w_ycopy(i):
        yp, peer = ypeer(i)
        return remote(w_y.at[yp], w_yin.at[y], wy.at[0, i], wy.at[1, i], peer)

    def w_acopy(i):
        return remote(w_a.at[zb], w_a.at[zb], wa.at[0, i], wa.at[1, i], bpeer(i))

    def w_bcopy(i):
        return remote(w_b.at[za], w_b.at[za], wb.at[0, i], wb.at[1, i], apeer(i))

    fourth = pl.ds(pl.multiple_of(y * quarter, 16), quarter)

    def g_y(i):
        part = w_all.at[core, cx, fourth]
        return remote(part, part, gy.at[0, i], gy.at[1, i], ypeer(i)[1])

    def g_x(i):
        part = w_all.at[core, cx]
        return remote(part, part, gx.at[0, i], gx.at[1, i], xpeer(i)[1])

    def g_core():
        part = w_all.at[core]
        return remote(part, part, gc.at[0], gc.at[1], other)

    def dr_ycopy(i):
        yp, peer = ypeer(i)
        return remote(dr_s.at[yp], dr_y.at[y], ry.at[0, i], ry.at[1, i], peer)

    def dr_zcopy(i):
        zp, peer = zpeer(i)
        return remote(dr_zs.at[zp], dr_z.at[z], rz.at[0, i], rz.at[1, i], peer)

    def ds_zcopy(c, i):
        zp, peer = zpeer(i)
        return remote(ds_zs.at[c, zp], ds_z.at[c, z], dz.at[0, c, i], dz.at[1, c, i], peer)

    def fold(c):
        for i in range(ny - 1):
            ds_ycopy(c, i).wait_recv()
        total = ds_ref[pl.ds(c * ny, ny), y].astype(F32)
        for i in range(ny - 1):
            total += ds_y[c, i].astype(F32)
        rows = nn(to_z, total.astype(BF).reshape(plan.tile, n)).astype(BF)
        ds_zs[c] = rows.reshape(nz, msg, n)
        loop(nz - 1, lambda i: ds_zcopy(c, i).start())
        ds_z[c, z] = ds_zs[c, z]

    w_core().start()
    scaled = d_normed * gain
    d_row = inv_std * (
        scaled
        - jnp.mean(scaled, axis=-1, keepdims=True)
        - normal * jnp.mean(scaled * normal, axis=-1, keepdims=True)
    )
    dr_s[...] = d_row.astype(BF).reshape(ny, blk, ch)
    for i in range(ny - 1):
        dr_ycopy(i).start()
    dr_y[y] = dr_s[y]

    w_core().wait_recv()
    w_x[...] = (wg[core].astype(F32) + w_cin[...].astype(F32)).astype(BF)
    for i in range(nx - 1):
        w_xcopy(i).start()
    w_xin[cx] = w_x[cx]

    half = (plan.chunks + 1) // 2
    for c in range(half):
        fold(c)
    for i in range(ny - 1):
        dr_ycopy(i).wait_recv()
    rows = nn(to_z, dr_y[...].reshape(plan.tile, ch)).astype(BF)
    dr_zs[...] = rows.reshape(nz, msg, ch)
    loop(nz - 1, lambda i: dr_zcopy(i).start())
    dr_z[z] = dr_zs[z]

    for i in range(nx - 1):
        w_xcopy(i).wait_recv()
    total = summed(w_xin, nx).astype(BF)
    for i in range(ny):
        w_y[i, :quarter] = total[i * quarter : (i + 1) * quarter]
        w_y[i, quarter:] = total[share:]
    for i in range(ny - 1):
        w_ycopy(i).start()
    w_yin[y] = w_y[y]

    for c in range(half, plan.chunks):
        fold(c)

    for i in range(ny - 1):
        w_ycopy(i).wait_recv()
    w_a[zb] = summed(w_yin, ny).astype(BF)
    for i in range(qb - 1):
        w_acopy(i).start()
    for i in range(qb - 1):
        w_acopy(i).wait_recv()
    w_b[za] = summed(w_a, qb).astype(BF)
    for i in range(qa - 1):
        w_bcopy(i).start()
    for i in range(qa - 1):
        w_bcopy(i).wait_recv()
    scale = 1.0 / (plan.nc * plan.dap)
    total = summed(w_b, qa)
    gain_out[...] = total[quarter:] * scale
    w_all[core, cx, fourth] = total[:quarter].astype(BF)
    for i in range(ny - 1):
        g_y(i).start()
    for c in range(half):
        loop(nz - 1, lambda i: ds_zcopy(c, i).wait_recv())
        db_out[pl.ds(c * ny, ny)] = summed(ds_z.at[c], nz).reshape(ny, plan.own, n)
    for i in range(ny - 1):
        g_y(i).wait_recv()
    for i in range(nx - 1):
        g_x(i).start()
    loop(nz - 1, lambda i: dr_zcopy(i).wait_recv())
    rows = nn(to_y, dr_z[...].reshape(plan.tile, ch)).astype(BF)
    dr_out[...] = rows.reshape(plan.dap, plan.own, ch)
    for c in range(half, plan.chunks):
        loop(nz - 1, lambda i: ds_zcopy(c, i).wait_recv())
        db_out[pl.ds(c * ny, ny)] = summed(ds_z.at[c], nz).reshape(ny, plan.own, n)
    for i in range(nx - 1):
        g_x(i).wait_recv()
    g_core().start()

    def take(t, half, rows, s, at):
        part = w_all[s // nx, s % nx, at].astype(F32) * scale
        cols = slice(half * LANES, (half + 1) * LANES)
        if t < 4:
            win_out[t, rows, cols] = part
        else:
            wout_out[rows, cols] = part

    for i in range(qa - 1):
        b_far(i).wait_send()
        w_bcopy(i).wait_send()
    for i in range(qb - 1):
        b_near(i).wait_send()
        w_acopy(i).wait_send()
    for i in range(ny - 1):
        x_y(i).wait_send()
        dr_ycopy(i).wait_send()
        w_ycopy(i).wait_send()
        g_y(i).wait_send()
        for c in range(plan.chunks):
            b_y(c, i).wait_send()
            ds_ycopy(c, i).wait_send()
    for i in range(nx - 1):
        w_xcopy(i).wait_send()
        g_x(i).wait_send()
    w_core().wait_send()
    loop(nz - 1, lambda i: x_z(i).wait_send())
    loop(nz - 1, lambda i: dr_zcopy(i).wait_send())
    for c in range(plan.chunks):
        loop(nz - 1, lambda i: ds_zcopy(c, i).wait_send())
    g_core().wait_recv()
    g_core().wait_send()
    keep(plan, take)


def dma(*shape):
    return pltpu.SemaphoreType.DMA(shape)


def on_device(plan, x, upstream, bias, extents, w_in, w_final, gain):
    ny, nz, nx, n, ch = plan.ny, plan.nz, plan.nx, plan.n, plan.c
    msg, blk, chunks, heads = plan.msg, plan.blk, plan.chunks, plan.heads
    total, part = plan.share + plan.extra, plan.quarter + plan.extra

    def buf(*shape, kind=BF):
        return pltpu.VMEM(shape, kind)

    d_rows, d_bias, d_in, d_out, gain_sum = pl.pallas_call(
        functools.partial(whole_kernel, plan),
        out_shape=(
            jax.ShapeDtypeStruct((plan.dap, plan.own, ch), BF),
            jax.ShapeDtypeStruct((heads, plan.own, n), F32),
            jax.ShapeDtypeStruct((4, ch, ch), F32),
            jax.ShapeDtypeStruct((ch, ch), F32),
            jax.ShapeDtypeStruct((plan.extra, LANES), F32),
        ),
        in_specs=[SMEM] + [ANY] * 6,
        out_specs=(VMEM,) * 5,
        scratch_shapes=[
            buf(plan.dap, plan.own, ch),
            buf(plan.dap, plan.own, ch),
            buf(heads, plan.own, n),
            buf(4, ch, ch),
            buf(ch, ch),
            buf(1, ch, kind=F32),
            buf(2, ny, blk, ch),
            buf(2, ny, blk, ch),
            buf(2, nz, msg, ch),
            buf(2, nz, msg, ch),
            buf(chunks, plan.qa, plan.qb, msg, n),
            buf(heads, n, n),
            buf(heads, ny, blk, n),
            buf(chunks, ny - 1, ny, blk, n),
            buf(chunks, nz, msg, n),
            buf(chunks, nz, msg, n),
            buf(ny, blk, ch),
            buf(ny, blk, ch),
            buf(nz, msg, ch),
            buf(nz, msg, ch),
            buf(2, nx, total, LANES),
            buf(nx, total, LANES),
            buf(nx, total, LANES),
            buf(nx, total, LANES),
            buf(ny, part, LANES),
            buf(ny, part, LANES),
            buf(plan.qb, part, LANES),
            buf(plan.qa, part, LANES),
            buf(2, nx, plan.share, LANES),
            dma(6),
            dma(2, ny - 1),
            dma(2, nz - 1),
            dma(2, plan.qa - 1),
            dma(2, plan.qb - 1),
            dma(2, chunks, ny - 1),
            dma(2, chunks, ny - 1),
            dma(2, chunks, nz - 1),
            dma(2, ny - 1),
            dma(2, nz - 1),
            dma(2),
            dma(2, nx - 1),
            dma(2, ny - 1),
            dma(2, plan.qb - 1),
            dma(2, plan.qa - 1),
            dma(2, ny - 1),
            dma(2, nx - 1),
            dma(2),
        ],
        compiler_params=pltpu.CompilerParams(
            collective_id=0, has_side_effects=True, vmem_limit_bytes=LIMIT
        ),
        name="row_attention_gradients",
    )(
        extents, x[0], upstream[0], bias[0], w_in, w_final, gain.reshape(1, ch)
    )
    return (
        d_rows[None],
        d_bias[None],
        d_in,
        d_out,
        gain_sum[:2].reshape(ch),
    )


def solution(mesh):
    split = P("crop", None, "dap", None)

    def whole(*arrays):
        plan = Plan(mesh, arrays[0].shape[2], arrays[0].shape[3], arrays[2].shape[1])
        return jax.shard_map(
            functools.partial(on_device, plan),
            mesh=mesh,
            in_specs=(split, split, split, P("crop"), P(), P(), P()),
            out_specs=(split, split, P(), P(), P()),
            check_vma=False,
        )(*arrays)

    return whole
```

time: 116 us -> 109 us (0.940)
  Pallas kernels: 105 us -> 99 us
    pallas_call x3 -> x1, Pallas kernels: 105 us -> 99 us  [on_device(): pl.pallas_call(functools.partial(whole_kernel, plan), out_shape=(jax.Shap...]
    unnamed x7 -> x16, local copies, waits for them, and re-layouts: 3.34 us -> 8.08 us
    reshape x5 -> x1, local copies, waits for them, and re-layouts: 3.93 us -> 0.56 us  [on_device(): return (d_rows[None], d_bias[None], d_in, d_out, gain_sum[:2].reshape(ch))]
    slice x3 -> x0, local copies, waits for them, and re-layouts: 1.28 us -> none  [the longest x1 1.06 us: on_device(): w_sum[:4]]
where the time goes in v2:
time: 109 us
  Pallas kernels  99 us (91%)
  local copies, waits for them, and re-layouts  8.65 us (8%)
  between operations  1.3 us (1%)
    pallas_call x1, Pallas kernels, on_device(): pl.pallas_call(functools.partial(whole_kernel, plan), out_shape=(jax.Shap...  99 us
    unnamed x16, local copies, waits for them, and re-layouts  8.08 us

profile of v2, /device:TPU:1, one launch (start us, length us, event | category | flops | bytes accessed | tf_op | source)
XLA Modules:
  0.0 108.9 jit_solution(8744638539131193719)
XLA Ops:
  1.3 0.0 copy-start.5
  1.3 0.7 copy-done.5
  2.0 0.0 copy-start
  2.0 1.0 copy-done
  3.0 0.0 copy-start.1
  3.0 0.9 copy-done.1
  3.9 0.0 copy-start.2
  3.9 0.9 copy-done.2
  4.8 0.0 copy-start.3
  4.8 0.9 copy-done.3
  5.7 0.0 copy-start.4
  5.7 0.7 copy-done.4
  6.4 99.0 %row_attention_gradients.1 = (bf16[64,4,256]{2,1,0:T(4,128)(2,1)S(1)}, f32[8,4,256]{2,1,0:T(4,128)S(1)}, f32[4,256,256]{2,1,0:T(8,128)S(1)}, f32[256,256]{1,0:T(8,128)S(1)}, f32[16,128]{1,0:T(8,128)S(1)}) custom-call(s32[1]{0:T(128)S(6)} %copy.16.ext_ref, bf16[64,4,256]{2,1,0:T(4,128)(2,1)S(1)} %bitcast.9, bf16[64,4,256]{2,1,0:T(4,128)(2,1)S(1)} %bitcast.10, ...), custom_call_target="tpu_custom_call" | custom-call | tf_op jit(solution)/shard_map/row_attention_gradients/pallas_call | solution.py:473
  105.4 0.6 slice_bitcast_fusion
  106.0 0.7 copy.17
  106.6 0.6 copy.18
  107.3 1.0 copy.19
  108.2 0.7 copy.20
Async XLA Ops:
  1.3 0.7 copy-start.5
  2.0 1.0 copy-start
  3.0 0.9 copy-start.1
  3.9 0.9 copy-start.2
  4.8 0.9 copy-start.3
  5.7 0.7 copy-start.4

commit v3 on v2

--- a/solution.py
+++ b/solution.py
@@ -16,7 +16,7 @@
 ANY = pl.BlockSpec(memory_space=pl.ANY)
 VMEM = pl.BlockSpec(memory_space=pltpu.VMEM)
 SMEM = pl.BlockSpec(memory_space=pltpu.SMEM)
-LIMIT = 44 * 1024 * 1024
+LIMIT = 60 * 1024 * 1024
 
 
 class Plan:
@@ -38,8 +38,8 @@
         self.chunks = heads // self.ny
         self.tile = self.ny * self.nz * self.own
         self.flat = 5 * channels * channels // LANES
-        self.share = self.flat // self.nc
-        self.quarter = self.share // self.ny
+        self.plane = self.nx * self.ny
+        self.share = self.flat // (2 * self.plane)
         self.extra = 16
 
 
@@ -114,9 +114,9 @@
     plan, ext_ref, x_hbm, g_hbm, b_hbm, win_hbm, wout_hbm, gain_hbm,
     dr_out, db_out, win_out, wout_out, gain_out,
     x_in, g_in, b_in, win_ref, wout_ref, gain_ref,
-    xg_s, xg_y, xg_zs, xg_z, b_z, bias_ref, ds_ref, ds_y, ds_zs, ds_z,
-    dr_s, dr_y, dr_zs, dr_z, wg, w_cin, w_x, w_xin, w_y, w_yin, w_a, w_b, w_all,
-    lsem, xy, xz, bf, bn, by, dy, dz, ry, rz, wc, wx, wy, wa, wb, gy, gx, gc,
+    xg_s, xg_y, xg_zs, xg_z, b_z, bias_ref, ds_ref, ds_y, ds_n, ds_nin, ds_f, ds_fin,
+    dr_s, dr_y, dr_zs, dr_z, wg, w_cin, w_p, w_pin, w_a, w_b, w_all,
+    lsem, xy, xz, bf, bn, by, dy, dn, df, ry, rz, wc, wp, wa, wb, gp, gc,
 ):
     y, z = place(plan)
     crop = lax.axis_index("crop")
@@ -124,7 +124,8 @@
     ny, nz, nx, blk, qa, qb = plan.ny, plan.nz, plan.nx, plan.blk, plan.qa, plan.qb
     za, zb = z // qb, z % qb
     n, ch, msg = plan.n, plan.c, plan.msg
-    share, quarter, extra = plan.share, plan.quarter, plan.extra
+    share, extra, plane = plan.share, plan.extra, plan.plane
+    spot = cx * ny + y
 
     def zpeer(i):
         step = (i + 1) // 2
@@ -135,15 +136,19 @@
         yp = lax.rem(y + i + 1, ny)
         return yp, {"dap": yp * nz + z}
 
-    def xpeer(i):
-        xp = lax.rem(cx + i + 1, nx)
-        return xp, {"crop": xp * 2 + core}
+    def ppeer(i):
+        to = lax.rem(spot + i + 1, plane)
+        return to, {"crop": (to // ny) * 2 + core, "dap": (to % ny) * nz + z}
 
     def apeer(i):
         return {"dap": y * nz + lax.rem(za + i + 1, qa) * qb + zb}
 
     def bpeer(i):
         return {"dap": y * nz + za * qb + lax.rem(zb + i + 1, qb)}
+
+    def xpeer(i):
+        xp = lax.rem(cx + i // ny + 1, nx)
+        return {"crop": xp * 2 + core, "dap": (i % ny) * nz + z}
 
     other = {"crop": cx * 2 + 1 - core}
 
@@ -161,8 +166,7 @@
     loop(nz - 1, lambda i: signal(zpeer(i)[1]))
     for i in range(ny - 1):
         signal(ypeer(i)[1])
-    for i in range(nx - 1):
-        signal(xpeer(i)[1])
+    loop(plane - ny, lambda i: signal(xpeer(i)))
     signal(other)
     for c in local[:3]:
         c.wait()
@@ -171,7 +175,7 @@
     xg_s[1] = g_in[...].reshape(ny, blk, ch)
     to_y = swap_matrix(plan, False)
     to_z = swap_matrix(plan, True)
-    pl.semaphore_wait(pltpu.get_barrier_semaphore(), nz + ny + nx - 2)
+    pl.semaphore_wait(pltpu.get_barrier_semaphore(), nz + plane - 1)
 
     def b_far(i):
         part = b_z.at[:, za, zb]
@@ -200,16 +204,16 @@
     for i in range(ny - 1):
         x_y(i).start()
     xg_y[:, y] = xg_s[:, y]
-    for i in range(qa - 1):
-        b_far(i).wait_recv()
-    for i in range(qb - 1):
-        b_near(i).start()
     for i in range(ny - 1):
         x_y(i).wait_recv()
     for t in range(2):
         rows = nn(to_z, xg_y[t].reshape(plan.tile, ch)).astype(BF)
         xg_zs[t] = rows.reshape(nz, msg, ch)
     loop(nz - 1, lambda i: x_z(i).start())
+    for i in range(qa - 1):
+        b_far(i).wait_recv()
+    for i in range(qb - 1):
+        b_near(i).start()
     xg_z[:, z] = xg_zs[:, z]
     for i in range(qb - 1):
         b_near(i).wait_recv()
@@ -282,7 +286,7 @@
     terms = [tn(normed, grads[p]).astype(BF) for p in range(4)] + [tn(gated, mg).astype(BF)]
 
     def put(t, half, rows, s, at):
-        wg[s // nx, s % nx, at] = terms[t][rows, half * LANES : (half + 1) * LANES]
+        wg[s // plane, s % plane, at] = terms[t][rows, half * LANES : (half + 1) * LANES]
 
     keep(plan, put)
     d_gain = jnp.sum(d_normed * normal, axis=0, keepdims=True)
@@ -290,19 +294,15 @@
     lo = jnp.broadcast_to(d_gain[:, :LANES], (extra, LANES))
     hi = jnp.broadcast_to(d_gain[:, LANES:], (extra, LANES))
     block = jnp.where(line == 0, lo, jnp.where(line == 1, hi, 0.0)).astype(BF)
-    for c in range(plan.nc):
-        wg[c // nx, c % nx, share:] = block
+    for core_of in range(2):
+        wg[core_of, :, share:] = jnp.broadcast_to(block[None], (plane, extra, LANES))
 
     def w_core():
         return remote(wg.at[1 - core], w_cin, wc.at[0], wc.at[1], other)
 
-    def w_xcopy(i):
-        xp, peer = xpeer(i)
-        return remote(w_x.at[xp], w_xin.at[cx], wx.at[0, i], wx.at[1, i], peer)
-
-    def w_ycopy(i):
-        yp, peer = ypeer(i)
-        return remote(w_y.at[yp], w_yin.at[y], wy.at[0, i], wy.at[1, i], peer)
+    def w_pcopy(i):
+        to, peer = ppeer(i)
+        return remote(w_p.at[to], w_pin.at[spot], wp.at[0, i], wp.at[1, i], peer)
 
     def w_acopy(i):
         return remote(w_a.at[zb], w_a.at[zb], wa.at[0, i], wa.at[1, i], bpeer(i))
@@ -310,15 +310,9 @@
     def w_bcopy(i):
         return remote(w_b.at[za], w_b.at[za], wb.at[0, i], wb.at[1, i], apeer(i))
 
-    fourth = pl.ds(pl.multiple_of(y * quarter, 16), quarter)
-
-    def g_y(i):
-        part = w_all.at[core, cx, fourth]
-        return remote(part, part, gy.at[0, i], gy.at[1, i], ypeer(i)[1])
-
-    def g_x(i):
-        part = w_all.at[core, cx]
-        return remote(part, part, gx.at[0, i], gx.at[1, i], xpeer(i)[1])
+    def g_p(i):
+        part = w_all.at[core, spot]
+        return remote(part, part, gp.at[0, i], gp.at[1, i], ppeer(i)[1])
 
     def g_core():
         part = w_all.at[core]
@@ -332,9 +326,14 @@
         zp, peer = zpeer(i)
         return remote(dr_zs.at[zp], dr_z.at[z], rz.at[0, i], rz.at[1, i], peer)
 
-    def ds_zcopy(c, i):
-        zp, peer = zpeer(i)
-        return remote(ds_zs.at[c, zp], ds_z.at[c, z], dz.at[0, c, i], dz.at[1, c, i], peer)
+    def ds_near(c, i):
+        bp = lax.rem(zb + i + 1, qb)
+        part = ds_n.at[c, :, bp]
+        return remote(part, ds_nin.at[c, i], dn.at[0, c, i], dn.at[1, c, i], bpeer(i))
+
+    def ds_far(i):
+        ap = lax.rem(za + i + 1, qa)
+        return remote(ds_f.at[:, ap], ds_fin.at[:, i], df.at[0, i], df.at[1, i], apeer(i))
 
     def fold(c):
         for i in range(ny - 1):
@@ -343,9 +342,9 @@
         for i in range(ny - 1):
             total += ds_y[c, i].astype(F32)
         rows = nn(to_z, total.astype(BF).reshape(plan.tile, n)).astype(BF)
-        ds_zs[c] = rows.reshape(nz, msg, n)
-        loop(nz - 1, lambda i: ds_zcopy(c, i).start())
-        ds_z[c, z] = ds_zs[c, z]
+        ds_n[c] = rows.reshape(qa, qb, msg, n)
+        for i in range(qb - 1):
+            ds_near(c, i).start()
 
     w_core().start()
     scaled = d_normed * gain
@@ -360,10 +359,9 @@
     dr_y[y] = dr_s[y]
 
     w_core().wait_recv()
-    w_x[...] = (wg[core].astype(F32) + w_cin[...].astype(F32)).astype(BF)
-    for i in range(nx - 1):
-        w_xcopy(i).start()
-    w_xin[cx] = w_x[cx]
+    w_p[...] = (wg[core].astype(F32) + w_cin[...].astype(F32)).astype(BF)
+    loop(plane - 1, lambda i: w_pcopy(i).start())
+    w_pin[spot] = w_p[spot]
 
     half = (plan.chunks + 1) // 2
     for c in range(half):
@@ -374,25 +372,22 @@
     dr_zs[...] = rows.reshape(nz, msg, ch)
     loop(nz - 1, lambda i: dr_zcopy(i).start())
     dr_z[z] = dr_zs[z]
-
-    for i in range(nx - 1):
-        w_xcopy(i).wait_recv()
-    total = summed(w_xin, nx).astype(BF)
-    for i in range(ny):
-        w_y[i, :quarter] = total[i * quarter : (i + 1) * quarter]
-        w_y[i, quarter:] = total[share:]
-    for i in range(ny - 1):
-        w_ycopy(i).start()
-    w_yin[y] = w_y[y]
-
     for c in range(half, plan.chunks):
         fold(c)
 
-    for i in range(ny - 1):
-        w_ycopy(i).wait_recv()
-    w_a[zb] = summed(w_yin, ny).astype(BF)
+    loop(plane - 1, lambda i: w_pcopy(i).wait_recv())
+    w_a[zb] = summed(w_pin, plane).astype(BF)
     for i in range(qb - 1):
         w_acopy(i).start()
+    for c in range(plan.chunks):
+        for i in range(qb - 1):
+            ds_near(c, i).wait_recv()
+        total = ds_n[c, :, zb].astype(F32)
+        for i in range(qb - 1):
+            total += ds_nin[c, i].astype(F32)
+        ds_f[c] = total.astype(BF)
+    for i in range(qa - 1):
+        ds_far(i).start()
     for i in range(qb - 1):
         w_acopy(i).wait_recv()
     w_b[za] = summed(w_a, qb).astype(BF)
@@ -402,29 +397,23 @@
         w_bcopy(i).wait_recv()
     scale = 1.0 / (plan.nc * plan.dap)
     total = summed(w_b, qa)
-    gain_out[...] = total[quarter:] * scale
-    w_all[core, cx, fourth] = total[:quarter].astype(BF)
-    for i in range(ny - 1):
-        g_y(i).start()
-    for c in range(half):
-        loop(nz - 1, lambda i: ds_zcopy(c, i).wait_recv())
-        db_out[pl.ds(c * ny, ny)] = summed(ds_z.at[c], nz).reshape(ny, plan.own, n)
-    for i in range(ny - 1):
-        g_y(i).wait_recv()
-    for i in range(nx - 1):
-        g_x(i).start()
+    w_all[core, spot] = total[:share].astype(BF)
+    loop(plane - 1, lambda i: g_p(i).start())
+    gain_out[...] = total[share:] * scale
     loop(nz - 1, lambda i: dr_zcopy(i).wait_recv())
     rows = nn(to_y, dr_z[...].reshape(plan.tile, ch)).astype(BF)
     dr_out[...] = rows.reshape(plan.dap, plan.own, ch)
-    for c in range(half, plan.chunks):
-        loop(nz - 1, lambda i: ds_zcopy(c, i).wait_recv())
-        db_out[pl.ds(c * ny, ny)] = summed(ds_z.at[c], nz).reshape(ny, plan.own, n)
-    for i in range(nx - 1):
-        g_x(i).wait_recv()
+    for i in range(qa - 1):
+        ds_far(i).wait_recv()
+    total = ds_f[:, za].astype(F32)
+    for i in range(qa - 1):
+        total += ds_fin[:, i].astype(F32)
+    db_out[...] = total.reshape(plan.heads, plan.own, n)
+    loop(plane - 1, lambda i: g_p(i).wait_recv())
     g_core().start()
 
     def take(t, half, rows, s, at):
-        part = w_all[s // nx, s % nx, at].astype(F32) * scale
+        part = w_all[s // plane, s % plane, at].astype(F32) * scale
         cols = slice(half * LANES, (half + 1) * LANES)
         if t < 4:
             win_out[t, rows, cols] = part
@@ -434,25 +423,23 @@
     for i in range(qa - 1):
         b_far(i).wait_send()
         w_bcopy(i).wait_send()
+        ds_far(i).wait_send()
     for i in range(qb - 1):
         b_near(i).wait_send()
         w_acopy(i).wait_send()
+        for c in range(plan.chunks):
+            ds_near(c, i).wait_send()
     for i in range(ny - 1):
         x_y(i).wait_send()
         dr_ycopy(i).wait_send()
-        w_ycopy(i).wait_send()
-        g_y(i).wait_send()
         for c in range(plan.chunks):
             b_y(c, i).wait_send()
             ds_ycopy(c, i).wait_send()
-    for i in range(nx - 1):
-        w_xcopy(i).wait_send()
-        g_x(i).wait_send()
+    loop(plane - 1, lambda i: w_pcopy(i).wait_send())
+    loop(plane - 1, lambda i: g_p(i).wait_send())
     w_core().wait_send()
     loop(nz - 1, lambda i: x_z(i).wait_send())
     loop(nz - 1, lambda i: dr_zcopy(i).wait_send())
-    for c in range(plan.chunks):
-        loop(nz - 1, lambda i: ds_zcopy(c, i).wait_send())
     g_core().wait_recv()
     g_core().wait_send()
     keep(plan, take)
@@ -463,9 +450,9 @@
 
 
 def on_device(plan, x, upstream, bias, extents, w_in, w_final, gain):
-    ny, nz, nx, n, ch = plan.ny, plan.nz, plan.nx, plan.n, plan.c
+    ny, nz, n, ch = plan.ny, plan.nz, plan.n, plan.c
     msg, blk, chunks, heads = plan.msg, plan.blk, plan.chunks, plan.heads
-    total, part = plan.share + plan.extra, plan.quarter + plan.extra
+    total, plane = plan.share + plan.extra, plan.plane
 
     def buf(*shape, kind=BF):
         return pltpu.VMEM(shape, kind)
@@ -496,21 +483,21 @@
             buf(heads, n, n),
             buf(heads, ny, blk, n),
             buf(chunks, ny - 1, ny, blk, n),
-            buf(chunks, nz, msg, n),
-            buf(chunks, nz, msg, n),
+            buf(chunks, plan.qa, plan.qb, msg, n),
+            buf(chunks, plan.qb - 1, plan.qa, msg, n),
+            buf(chunks, plan.qa, msg, n),
+            buf(chunks, plan.qa - 1, msg, n),
             buf(ny, blk, ch),
             buf(ny, blk, ch),
             buf(nz, msg, ch),
             buf(nz, msg, ch),
-            buf(2, nx, total, LANES),
-            buf(nx, total, LANES),
-            buf(nx, total, LANES),
-            buf(nx, total, LANES),
-            buf(ny, part, LANES),
-            buf(ny, part, LANES),
-            buf(plan.qb, part, LANES),
-            buf(plan.qa, part, LANES),
-            buf(2, nx, plan.share, LANES),
+            buf(2, plane, total, LANES),
+            buf(plane, total, LANES),
+            buf(plane, total, LANES),
+            buf(plane, total, LANES),
+            buf(plan.qb, total, LANES),
+            buf(plan.qa, total, LANES),
+            buf(2, plane, plan.share, LANES),
             dma(6),
             dma(2, ny - 1),
             dma(2, nz - 1),
@@ -518,16 +505,15 @@
             dma(2, plan.qb - 1),
             dma(2, chunks, ny - 1),
             dma(2, chunks, ny - 1),
-            dma(2, chunks, nz - 1),
+            dma(2, chunks, plan.qb - 1),
+            dma(2, plan.qa - 1),
             dma(2, ny - 1),
             dma(2, nz - 1),
             dma(2),
-            dma(2, nx - 1),
-            dma(2, ny - 1),
+            dma(2, plane - 1),
             dma(2, plan.qb - 1),
             dma(2, plan.qa - 1),
-            dma(2, ny - 1),
-            dma(2, nx - 1),
+            dma(2, plane - 1),
             dma(2),
         ],
         compiler_params=pltpu.CompilerParams(

time: 109 us -> 110 us (level)
  Pallas kernels: 99 us -> 102 us
  local copies, waits for them, and re-layouts: 8.65 us -> 6.5 us
    pallas_call x1, Pallas kernels: 99 us -> 102 us  [on_device(): pl.pallas_call(functools.partial(whole_kernel, plan), out_shape=(jax.Shap...]
    unnamed x16 -> x8, local copies, waits for them, and re-layouts: 8.08 us -> 5.26 us
where the time goes in v3:
time: 110 us
  Pallas kernels  102 us (93%)
  local copies, waits for them, and re-layouts  6.5 us (6%)
  between operations  1.29 us (1%)
    pallas_call x1, Pallas kernels, on_device(): pl.pallas_call(functools.partial(whole_kernel, plan), out_shape=(jax.Shap...  102 us
    unnamed x8, local copies, waits for them, and re-layouts  5.26 us

profile of v3, /device:TPU:1, one launch (start us, length us, event | category | flops | bytes accessed | tf_op | source)
XLA Modules:
  0.0 110.0 jit_solution(2373927277229967532)
XLA Ops:
  1.3 102.2 %row_attention_gradients.1 = (bf16[64,4,256]{2,1,0:T(4,128)(2,1)}, f32[8,4,256]{2,1,0:T(4,128)}, f32[4,256,256]{2,1,0:T(8,128)}, f32[256,256]{1,0:T(8,128)}, f32[16,128]{1,0:T(8,128)}) custom-call(s32[1]{0:T(128)S(6)} %copy.16.ext_ref, bf16[64,4,256]{2,1,0:T(4,128)(2,1)} %bitcast.9, bf16[64,4,256]{2,1,0:T(4,128)(2,1)} %bitcast.10, ...), custom_call_target="tpu_custom_call" | custom-call | tf_op jit(solution)/shard_map/row_attention_gradients/pallas_call | solution.py:460
  103.5 1.2 %slice_bitcast_fusion = f32[256]{0:T(256)} fusion(f32[16,128]{1,0:T(8,128)} %get-tuple-element.14), kind=kLoop, calls=%fused_computation | loop fusion | bytes 2048 | tf_op jit(solution)/shard_map/reshape | solution.py:531
  104.7 0.0 copy-start.1
  104.7 1.6 %copy.17 = bf16[1,64,4,256]{3,2,1,0:T(4,128)(2,1)} copy(bf16[1,64,4,256]{3,2,1,0:T(4,128)(2,1)} %bitcast.8) | data formatting | bytes 262144
  106.4 0.0 copy-done.1
  106.4 0.6 copy.18
  107.0 0.0 copy-start
  107.0 2.3 %copy.19 = f32[4,256,256]{2,1,0:T(8,128)} copy(f32[4,256,256]{2,1,0:T(8,128)} %get-tuple-element.22) | data formatting | bytes 2097152
  109.3 0.0 copy-done
  109.3 0.7 copy.20
Async XLA Ops:
  104.7 1.6 %copy-start.1 = (f32[8,4,256]{2,1,0:T(4,128)S(1)}, f32[8,4,256]{2,1,0:T(4,128)}, u32[]{:S(2)}) copy-start(f32[8,4,256]{2,1,0:T(4,128)} %get-tuple-element.11) | copy-start | bytes 98308
  107.0 2.3 %copy-start = (f32[256,256]{1,0:T(8,128)S(1)}, f32[256,256]{1,0:T(8,128)}, u32[]{:S(2)}) copy-start(f32[256,256]{1,0:T(8,128)} %get-tuple-element.23) | copy-start | bytes 786436

commit v4 on v3

--- a/solution.py
+++ b/solution.py
@@ -17,6 +17,7 @@
 VMEM = pl.BlockSpec(memory_space=pltpu.VMEM)
 SMEM = pl.BlockSpec(memory_space=pltpu.SMEM)
 LIMIT = 60 * 1024 * 1024
+EARLY = 5
 
 
 class Plan:
@@ -86,8 +87,20 @@
     )
 
 
-def loop(count, body):
-    lax.fori_loop(0, count, lambda i, c: (body(i), c)[1], 0)
+class Exchange:
+    def __init__(self, make, count, like, sems):
+        self.make, self.count, self.like, self.sems = make, count, like, sems
+
+    def start(self, low=0, high=None):
+        for i in range(low, self.count if high is None else high):
+            src, dst, peer = self.make(i)
+            remote(src, dst, self.sems.at[0], self.sems.at[1], peer).start()
+
+    def received(self):
+        pltpu.make_async_copy(self.like, self.like, self.sems.at[1]).wait()
+
+    def sent(self):
+        pltpu.make_async_copy(self.like, self.like, self.sems.at[0]).wait()
 
 
 def keep(plan, put):
@@ -112,11 +125,11 @@
 
 def whole_kernel(
     plan, ext_ref, x_hbm, g_hbm, b_hbm, win_hbm, wout_hbm, gain_hbm,
-    dr_out, db_out, win_out, wout_out, gain_out,
+    dr_out, db_out, w_all, gain_out,
     x_in, g_in, b_in, win_ref, wout_ref, gain_ref,
-    xg_s, xg_y, xg_zs, xg_z, b_z, bias_ref, ds_ref, ds_y, ds_n, ds_nin, ds_f, ds_fin,
-    dr_s, dr_y, dr_zs, dr_z, wg, w_cin, w_p, w_pin, w_a, w_b, w_all,
-    lsem, xy, xz, bf, bn, by, dy, dn, df, ry, rz, wc, wp, wa, wb, gp, gc,
+    xg_s, xg_y, xg_zs, xg_z, b_z, bias_ref, ds_ref, ds_y, z_out, z_in,
+    dr_s, dr_y, wg, w_cin, w_p, w_pin, w_a, w_b,
+    lsem, xy, xz, bf, bn, by, dy, z1, z2, ry, wc, wp, wa, wb, gp, gc,
 ):
     y, z = place(plan)
     crop = lax.axis_index("crop")
@@ -163,10 +176,12 @@
     ]
     for c in local:
         c.start()
-    loop(nz - 1, lambda i: signal(zpeer(i)[1]))
+    for i in range(nz - 1):
+        signal(zpeer(i)[1])
     for i in range(ny - 1):
         signal(ypeer(i)[1])
-    loop(plane - ny, lambda i: signal(xpeer(i)))
+    for i in range(plane - ny):
+        signal(xpeer(i))
     signal(other)
     for c in local[:3]:
         c.wait()
@@ -179,52 +194,58 @@
 
     def b_far(i):
         part = b_z.at[:, za, zb]
-        return remote(part, part, bf.at[0, i], bf.at[1, i], apeer(i))
+        return part, part, apeer(i)
 
     def b_near(i):
         part = b_z.at[:, :, zb]
-        return remote(part, part, bn.at[0, i], bn.at[1, i], bpeer(i))
+        return part, part, bpeer(i)
 
     mine = pl.ds(pl.multiple_of(y * blk, blk), blk)
 
-    def b_y(c, i):
-        part = bias_ref.at[pl.ds(c * ny, ny), mine]
-        return remote(part, part, by.at[0, c, i], by.at[1, c, i], ypeer(i)[1])
+    def bias_y(c):
+        heads = pl.ds(c * ny, ny)
+
+        def b_y(i):
+            part = bias_ref.at[heads, mine]
+            return part, part, ypeer(i)[1]
+
+        return Exchange(b_y, ny - 1, bias_ref.at[heads, pl.ds(0, (ny - 1) * blk)], by.at[c])
 
     def x_y(i):
         yp, peer = ypeer(i)
-        return remote(xg_s.at[:, yp], xg_y.at[:, y], xy.at[0, i], xy.at[1, i], peer)
+        return xg_s.at[:, yp], xg_y.at[:, y], peer
 
     def x_z(i):
         zp, peer = zpeer(i)
-        return remote(xg_zs.at[:, zp], xg_z.at[:, z], xz.at[0, i], xz.at[1, i], peer)
-
-    for i in range(qa - 1):
-        b_far(i).start()
-    for i in range(ny - 1):
-        x_y(i).start()
+        return xg_zs.at[:, zp], xg_z.at[:, z], peer
+
+    far = Exchange(b_far, qa - 1, b_z.at[:, pl.ds(0, qa - 1), 0], bf)
+    near = Exchange(b_near, qb - 1, b_z.at[:, :, pl.ds(0, qb - 1)], bn)
+    by_y = [bias_y(c) for c in range(plan.chunks)]
+    rows_y = Exchange(x_y, ny - 1, xg_y.at[:, pl.ds(0, ny - 1)], xy)
+    rows_z = Exchange(x_z, nz - 1, xg_z.at[:, pl.ds(0, nz - 1)], xz)
+
+    far.start()
+    rows_y.start()
     xg_y[:, y] = xg_s[:, y]
-    for i in range(ny - 1):
-        x_y(i).wait_recv()
+    rows_y.received()
     for t in range(2):
         rows = nn(to_z, xg_y[t].reshape(plan.tile, ch)).astype(BF)
         xg_zs[t] = rows.reshape(nz, msg, ch)
-    loop(nz - 1, lambda i: x_z(i).start())
-    for i in range(qa - 1):
-        b_far(i).wait_recv()
-    for i in range(qb - 1):
-        b_near(i).start()
+    early = EARLY * (nz - 1) // 15
+    rows_z.start(0, early)
+    far.received()
+    near.start()
+    rows_z.start(early)
     xg_z[:, z] = xg_zs[:, z]
-    for i in range(qb - 1):
-        b_near(i).wait_recv()
+    near.received()
     for c in range(plan.chunks):
         rows = nn(to_y, b_z[c].reshape(plan.tile, n)).astype(BF)
         bias_ref[pl.ds(c * ny, ny), mine] = rows.reshape(ny, blk, n)
-        for i in range(ny - 1):
-            b_y(c, i).start()
+        by_y[c].start()
     for c in local[3:]:
         c.wait()
-    loop(nz - 1, lambda i: x_z(i).wait_recv())
+    rows_z.received()
 
     size = ch // plan.heads
     mult = 1.0 / math.sqrt(size)
@@ -246,15 +267,17 @@
     head_of = lax.broadcasted_iota(jnp.int32, (1, ch), 1) // size
     att = dv = dq = dk = jnp.zeros((n, ch), F32)
 
-    def ds_ycopy(c, i):
-        yp, peer = ypeer(i)
-        part = ds_ref.at[pl.ds(c * ny, ny), yp]
-        return remote(part, ds_y.at[c, i], dy.at[0, c, i], dy.at[1, c, i], peer)
-
+    def scores_y(c):
+        def ds_y_(i):
+            yp, peer = ypeer(i)
+            return ds_ref.at[pl.ds(c * ny, ny), yp], ds_y.at[c, i], peer
+
+        return Exchange(ds_y_, ny - 1, ds_y.at[c], dy.at[c])
+
+    ds_by_y = [scores_y(c) for c in range(plan.chunks)]
     for h in range(plan.heads):
         if h % ny == 0:
-            for i in range(ny - 1):
-                b_y(h // ny, i).wait_recv()
+            by_y[h // ny].received()
         own = jnp.where(head_of == h, 1.0, 0.0).astype(BF)
         qh, kh, vh, dah = q * own, k * own, v * own, da * own
         scores = nt(qh, k) * mult + bias_ref[h].astype(F32)
@@ -270,9 +293,8 @@
         dv += tn(pb, dah)
         dq += nn(dsb, kh)
         dk += tn(dsb, qh)
-        if h % ny == ny - 1:
-            for i in range(ny - 1):
-                ds_ycopy(h // ny, i).start()
+        if h % ny == ny - 1 and h < plan.heads - 1:
+            ds_by_y[h // ny].start()
     gated = (att * gate).astype(BF)
     grads = [
         (dq * mult).astype(BF),
@@ -297,56 +319,62 @@
     for core_of in range(2):
         wg[core_of, :, share:] = jnp.broadcast_to(block[None], (plane, extra, LANES))
 
-    def w_core():
-        return remote(wg.at[1 - core], w_cin, wc.at[0], wc.at[1], other)
-
-    def w_pcopy(i):
+    def w_c(i):
+        return wg.at[1 - core], w_cin, other
+
+    def w_plane(i):
         to, peer = ppeer(i)
-        return remote(w_p.at[to], w_pin.at[spot], wp.at[0, i], wp.at[1, i], peer)
-
-    def w_acopy(i):
-        return remote(w_a.at[zb], w_a.at[zb], wa.at[0, i], wa.at[1, i], bpeer(i))
-
-    def w_bcopy(i):
-        return remote(w_b.at[za], w_b.at[za], wb.at[0, i], wb.at[1, i], apeer(i))
-
-    def g_p(i):
+        return w_p.at[to], w_pin.at[spot], peer
+
+    def w_near(i):
+        return w_a.at[zb], w_a.at[zb], bpeer(i)
+
+    def w_far(i):
+        return w_b.at[za], w_b.at[za], apeer(i)
+
+    def g_plane(i):
         part = w_all.at[core, spot]
-        return remote(part, part, gp.at[0, i], gp.at[1, i], ppeer(i)[1])
-
-    def g_core():
-        part = w_all.at[core]
-        return remote(part, part, gc.at[0], gc.at[1], other)
-
-    def dr_ycopy(i):
+        return part, part, ppeer(i)[1]
+
+    def g_core(i):
+        return w_all.at[core], w_all.at[core], other
+
+    by_core = Exchange(w_c, 1, w_cin, wc)
+    by_plane = Exchange(w_plane, plane - 1, w_pin.at[pl.ds(0, plane - 1)], wp)
+    by_near = Exchange(w_near, qb - 1, w_a.at[pl.ds(0, qb - 1)], wa)
+    by_far = Exchange(w_far, qa - 1, w_b.at[pl.ds(0, qa - 1)], wb)
+    to_plane = Exchange(g_plane, plane - 1, w_all.at[0, pl.ds(0, plane - 1)], gp)
+    to_core = Exchange(g_core, 1, w_all.at[0], gc)
+
+    def dr_y_(i):
         yp, peer = ypeer(i)
-        return remote(dr_s.at[yp], dr_y.at[y], ry.at[0, i], ry.at[1, i], peer)
-
-    def dr_zcopy(i):
+        return dr_s.at[yp], dr_y.at[y], peer
+
+    def first_z(i):
         zp, peer = zpeer(i)
-        return remote(dr_zs.at[zp], dr_z.at[z], rz.at[0, i], rz.at[1, i], peer)
-
-    def ds_near(c, i):
-        bp = lax.rem(zb + i + 1, qb)
-        part = ds_n.at[c, :, bp]
-        return remote(part, ds_nin.at[c, i], dn.at[0, c, i], dn.at[1, c, i], bpeer(i))
-
-    def ds_far(i):
-        ap = lax.rem(za + i + 1, qa)
-        return remote(ds_f.at[:, ap], ds_fin.at[:, i], df.at[0, i], df.at[1, i], apeer(i))
+        return z_out.at[zp, pl.ds(0, half)], z_in.at[z, pl.ds(0, half)], peer
+
+    def last_z(i):
+        zp, peer = zpeer(i)
+        part = pl.ds(half, plan.chunks + 1 - half)
+        return z_out.at[zp, part], z_in.at[z, part], peer
+
+    half = plan.chunks // 2
+    others = pl.ds(0, nz - 1)
+    dr_by_y = Exchange(dr_y_, ny - 1, dr_y.at[pl.ds(0, ny - 1)], ry)
+    z_first = Exchange(first_z, nz - 1, z_in.at[others, pl.ds(0, half)], z1)
+    z_last = Exchange(last_z, nz - 1, z_in.at[others, pl.ds(half, plan.chunks + 1 - half)], z2)
 
     def fold(c):
-        for i in range(ny - 1):
-            ds_ycopy(c, i).wait_recv()
+        ds_by_y[c].received()
         total = ds_ref[pl.ds(c * ny, ny), y].astype(F32)
         for i in range(ny - 1):
             total += ds_y[c, i].astype(F32)
         rows = nn(to_z, total.astype(BF).reshape(plan.tile, n)).astype(BF)
-        ds_n[c] = rows.reshape(qa, qb, msg, n)
-        for i in range(qb - 1):
-            ds_near(c, i).start()
-
-    w_core().start()
+        z_out[:, c] = rows.reshape(nz, msg, n)
+
+    by_core.start()
+    ds_by_y[-1].start()
     scaled = d_normed * gain
     d_row = inv_std * (
         scaled
@@ -354,94 +382,72 @@
         - normal * jnp.mean(scaled * normal, axis=-1, keepdims=True)
     )
     dr_s[...] = d_row.astype(BF).reshape(ny, blk, ch)
-    for i in range(ny - 1):
-        dr_ycopy(i).start()
+    dr_by_y.start()
     dr_y[y] = dr_s[y]
 
-    w_core().wait_recv()
+    by_core.received()
     w_p[...] = (wg[core].astype(F32) + w_cin[...].astype(F32)).astype(BF)
-    loop(plane - 1, lambda i: w_pcopy(i).start())
+    by_plane.start()
     w_pin[spot] = w_p[spot]
-
-    half = (plan.chunks + 1) // 2
     for c in range(half):
         fold(c)
-    for i in range(ny - 1):
-        dr_ycopy(i).wait_recv()
-    rows = nn(to_z, dr_y[...].reshape(plan.tile, ch)).astype(BF)
-    dr_zs[...] = rows.reshape(nz, msg, ch)
-    loop(nz - 1, lambda i: dr_zcopy(i).start())
-    dr_z[z] = dr_zs[z]
+    z_first.start()
     for c in range(half, plan.chunks):
         fold(c)
-
-    loop(plane - 1, lambda i: w_pcopy(i).wait_recv())
+    dr_by_y.received()
+    rows = nn(to_z, dr_y[...].reshape(plan.tile, ch)).astype(BF)
+    z_out[:, plan.chunks] = rows.reshape(nz, msg, ch)
+    z_last.start()
+    z_in[z] = z_out[z]
+
+    by_plane.received()
     w_a[zb] = summed(w_pin, plane).astype(BF)
-    for i in range(qb - 1):
-        w_acopy(i).start()
-    for c in range(plan.chunks):
-        for i in range(qb - 1):
-            ds_near(c, i).wait_recv()
-        total = ds_n[c, :, zb].astype(F32)
-        for i in range(qb - 1):
-            total += ds_nin[c, i].astype(F32)
-        ds_f[c] = total.astype(BF)
-    for i in range(qa - 1):
-        ds_far(i).start()
-    for i in range(qb - 1):
-        w_acopy(i).wait_recv()
+    by_near.start()
+    by_near.received()
     w_b[za] = summed(w_a, qb).astype(BF)
-    for i in range(qa - 1):
-        w_bcopy(i).start()
-    for i in range(qa - 1):
-        w_bcopy(i).wait_recv()
+    by_far.start()
+    by_far.received()
     scale = 1.0 / (plan.nc * plan.dap)
     total = summed(w_b, qa)
     w_all[core, spot] = total[:share].astype(BF)
-    loop(plane - 1, lambda i: g_p(i).start())
+    to_plane.start()
     gain_out[...] = total[share:] * scale
-    loop(nz - 1, lambda i: dr_zcopy(i).wait_recv())
-    rows = nn(to_y, dr_z[...].reshape(plan.tile, ch)).astype(BF)
-    dr_out[...] = rows.reshape(plan.dap, plan.own, ch)
-    for i in range(qa - 1):
-        ds_far(i).wait_recv()
-    total = ds_f[:, za].astype(F32)
-    for i in range(qa - 1):
-        total += ds_fin[:, i].astype(F32)
-    db_out[...] = total.reshape(plan.heads, plan.own, n)
-    loop(plane - 1, lambda i: g_p(i).wait_recv())
-    g_core().start()
+    z_first.received()
+    z_last.received()
+    for c in range(plan.chunks):
+        total = z_in[0, c].astype(F32)
+        for i in range(1, nz):
+            total += z_in[i, c].astype(F32)
+        db_out[c] = total
+    rows = nn(to_y, z_in[:, plan.chunks].reshape(plan.tile, ch)).astype(BF)
+    dr_out[...] = rows
+    to_plane.received()
+    to_core.start()
+
+    exchanges = [far, near, *by_y, rows_y, rows_z, *ds_by_y, by_core, by_plane, by_near, by_far]
+    for e in exchanges + [to_plane, dr_by_y, z_first, z_last]:
+        e.sent()
+    to_core.received()
+    to_core.sent()
+
+
+def unpack_kernel(
+    plan, dr_ref, db_ref, w_all, gain_ref, dr_out, db_out, win_out, wout_out, gain_out
+):
+    scale = 1.0 / (plan.nc * plan.dap)
+    dr_out[...] = dr_ref[...].reshape(dr_out.shape)
+    db_out[...] = db_ref[...].reshape(db_out.shape)
+    gain_out[:, :LANES] = gain_ref[0:1]
+    gain_out[:, LANES:] = gain_ref[1:2]
 
     def take(t, half, rows, s, at):
-        part = w_all[s // plane, s % plane, at].astype(F32) * scale
+        part = w_all[s // plan.plane, s % plan.plane, at].astype(F32) * scale
         cols = slice(half * LANES, (half + 1) * LANES)
         if t < 4:
             win_out[t, rows, cols] = part
         else:
             wout_out[rows, cols] = part
 
-    for i in range(qa - 1):
-        b_far(i).wait_send()
-        w_bcopy(i).wait_send()
-        ds_far(i).wait_send()
-    for i in range(qb - 1):
-        b_near(i).wait_send()
-        w_acopy(i).wait_send()
-        for c in range(plan.chunks):
-            ds_near(c, i).wait_send()
-    for i in range(ny - 1):
-        x_y(i).wait_send()
-        dr_ycopy(i).wait_send()
-        for c in range(plan.chunks):
-            b_y(c, i).wait_send()
-            ds_ycopy(c, i).wait_send()
-    loop(plane - 1, lambda i: w_pcopy(i).wait_send())
-    loop(plane - 1, lambda i: g_p(i).wait_send())
-    w_core().wait_send()
-    loop(nz - 1, lambda i: x_z(i).wait_send())
-    loop(nz - 1, lambda i: dr_zcopy(i).wait_send())
-    g_core().wait_recv()
-    g_core().wait_send()
     keep(plan, take)
 
 
@@ -457,17 +463,16 @@
     def buf(*shape, kind=BF):
         return pltpu.VMEM(shape, kind)
 
-    d_rows, d_bias, d_in, d_out, gain_sum = pl.pallas_call(
+    sums = pl.pallas_call(
         functools.partial(whole_kernel, plan),
         out_shape=(
-            jax.ShapeDtypeStruct((plan.dap, plan.own, ch), BF),
-            jax.ShapeDtypeStruct((heads, plan.own, n), F32),
-            jax.ShapeDtypeStruct((4, ch, ch), F32),
-            jax.ShapeDtypeStruct((ch, ch), F32),
+            jax.ShapeDtypeStruct((n, ch), BF),
+            jax.ShapeDtypeStruct((chunks, msg, n), F32),
+            jax.ShapeDtypeStruct((2, plane, plan.share, LANES), BF),
             jax.ShapeDtypeStruct((plan.extra, LANES), F32),
         ),
         in_specs=[SMEM] + [ANY] * 6,
-        out_specs=(VMEM,) * 5,
+        out_specs=(VMEM,) * 4,
         scratch_shapes=[
             buf(plan.dap, plan.own, ch),
             buf(plan.dap, plan.own, ch),
@@ -483,38 +488,24 @@
             buf(heads, n, n),
             buf(heads, ny, blk, n),
             buf(chunks, ny - 1, ny, blk, n),
-            buf(chunks, plan.qa, plan.qb, msg, n),
-            buf(chunks, plan.qb - 1, plan.qa, msg, n),
-            buf(chunks, plan.qa, msg, n),
-            buf(chunks, plan.qa - 1, msg, n),
+            buf(nz, chunks + 1, msg, n),
+            buf(nz, chunks + 1, msg, n),
             buf(ny, blk, ch),
             buf(ny, blk, ch),
-            buf(nz, msg, ch),
-            buf(nz, msg, ch),
             buf(2, plane, total, LANES),
             buf(plane, total, LANES),
             buf(plane, total, LANES),
             buf(plane, total, LANES),
             buf(plan.qb, total, LANES),
             buf(plan.qa, total, LANES),
-            buf(2, plane, plan.share, LANES),
             dma(6),
-            dma(2, ny - 1),
-            dma(2, nz - 1),
-            dma(2, plan.qa - 1),
-            dma(2, plan.qb - 1),
-            dma(2, chunks, ny - 1),
-            dma(2, chunks, ny - 1),
-            dma(2, chunks, plan.qb - 1),
-            dma(2, plan.qa - 1),
-            dma(2, ny - 1),
-            dma(2, nz - 1),
             dma(2),
-            dma(2, plane - 1),
-            dma(2, plan.qb - 1),
-            dma(2, plan.qa - 1),
-            dma(2, plane - 1),
             dma(2),
+            dma(2),
+            dma(2),
+            dma(chunks, 2),
+            dma(chunks, 2),
+            *[dma(2)] * 9,
         ],
         compiler_params=pltpu.CompilerParams(
             collective_id=0, has_side_effects=True, vmem_limit_bytes=LIMIT
@@ -523,13 +514,21 @@
     )(
         extents, x[0], upstream[0], bias[0], w_in, w_final, gain.reshape(1, ch)
     )
-    return (
-        d_rows[None],
-        d_bias[None],
-        d_in,
-        d_out,
-        gain_sum[:2].reshape(ch),
-    )
+    d_rows, d_bias, d_in, d_out, d_gain = pl.pallas_call(
+        functools.partial(unpack_kernel, plan),
+        out_shape=(
+            jax.ShapeDtypeStruct((plan.dap, plan.own, ch), BF),
+            jax.ShapeDtypeStruct((heads, plan.own, n), F32),
+            jax.ShapeDtypeStruct((4, ch, ch), F32),
+            jax.ShapeDtypeStruct((ch, ch), F32),
+            jax.ShapeDtypeStruct((1, ch), F32),
+        ),
+        in_specs=[VMEM] * 4,
+        out_specs=(VMEM,) * 5,
+        compiler_params=pltpu.CompilerParams(vmem_limit_bytes=LIMIT),
+        name="unpack_gradients",
+    )(*sums)
+    return (d_rows[None], d_bias[None], d_in, d_out, d_gain.reshape(ch))
 
 
 def solution(mesh):

time: 110 us -> 100 us (0.909)
  local copies, waits for them, and re-layouts: 6.5 us -> 0 us
  Pallas kernels: 102 us -> 98.7 us
    pallas_call x1, Pallas kernels: 102 us -> 96.4 us  [on_device(): pl.pallas_call(functools.partial(whole_kernel, plan), out_shape=(jax.Shap...]
    unnamed x8 -> x0, local copies, waits for them, and re-layouts: 5.26 us -> none
    pallas_call x0 -> x1, Pallas kernels: none -> 2.32 us  [on_device(): pl.pallas_call(functools.partial(unpack_kernel, plan), out_shape=(jax.Sha...]
    reshape x1 -> x0, local copies, waits for them, and re-layouts: 1.24 us -> none  [on_device(): return (d_rows[None], d_bias[None], d_in, d_out, gain_sum[:2].reshape(ch))]
where the time goes in v4:
time: 100 us
  Pallas kernels  98.7 us (99%)
  between operations  1.29 us (1%)
    pallas_call x1, Pallas kernels, on_device(): pl.pallas_call(functools.partial(whole_kernel, plan), out_shape=(jax.Shap...  96.4 us
    pallas_call x1, Pallas kernels, on_device(): pl.pallas_call(functools.partial(unpack_kernel, plan), out_shape=(jax.Sha...  2.32 us

profile of v4, /device:TPU:1, one launch (start us, length us, event | category | flops | bytes accessed | tf_op | source)
XLA Modules:
  0.0 100.0 jit_solution(11244049140174477811)
XLA Ops:
  1.3 96.4 %row_attention_gradients.1 = (bf16[256,256]{1,0:T(8,128)(2,1)}, f32[2,16,256]{2,1,0:T(8,128)}, bf16[2,16,80,128]{3,2,1,0:T(8,128)(2,1)}, f32[16,128]{1,0:T(8,128)}) custom-call(s32[1]{0:T(128)S(6)} %copy.12.ext_ref, bf16[64,4,256]{2,1,0:T(4,128)(2,1)} %bitcast.7, bf16[64,4,256]{2,1,0:T(4,128)(2,1)} %bitcast.8, bf16[8,4,256]{2,1,0:T(4,128)(2,1)} %bitcast.9, ...), custom_call_target="tpu_custom_call" | custom-call | tf_op jit(solution)/shard_map/row_attention_gradients/pallas_call | solution.py:466
  97.7 2.3 %unpack_gradients.1 = (bf16[64,4,256]{2,1,0:T(4,128)(2,1)}, f32[8,4,256]{2,1,0:T(4,128)}, f32[4,256,256]{2,1,0:T(8,128)}, f32[256,256]{1,0:T(8,128)}, f32[1,256]{1,0:T(1,128)}) custom-call(bf16[256,256]{1,0:T(8,128)(2,1)} %get-tuple-element.14.dr_ref, f32[2,16,256]{2,1,0:T(8,128)} %get-tuple-element.15.db_ref, ...), custom_call_target="tpu_custom_call" | custom-call | tf_op jit(solution)/shard_map/unpack_gradients/pallas_call | solution.py:517

commit v5 on v4

--- a/solution.py
+++ b/solution.py
@@ -17,7 +17,6 @@
 VMEM = pl.BlockSpec(memory_space=pltpu.VMEM)
 SMEM = pl.BlockSpec(memory_space=pltpu.SMEM)
 LIMIT = 60 * 1024 * 1024
-EARLY = 5
 
 
 class Plan:
@@ -228,16 +227,14 @@
     far.start()
     rows_y.start()
     xg_y[:, y] = xg_s[:, y]
+    far.received()
+    near.start()
     rows_y.received()
     for t in range(2):
         rows = nn(to_z, xg_y[t].reshape(plan.tile, ch)).astype(BF)
         xg_zs[t] = rows.reshape(nz, msg, ch)
-    early = EARLY * (nz - 1) // 15
-    rows_z.start(0, early)
-    far.received()
-    near.start()
-    rows_z.start(early)
     xg_z[:, z] = xg_zs[:, z]
+    rows_z.start()
     near.received()
     for c in range(plan.chunks):
         rows = nn(to_y, b_z[c].reshape(plan.tile, n)).astype(BF)
@@ -397,7 +394,6 @@
     dr_by_y.received()
     rows = nn(to_z, dr_y[...].reshape(plan.tile, ch)).astype(BF)
     z_out[:, plan.chunks] = rows.reshape(nz, msg, ch)
-    z_last.start()
     z_in[z] = z_out[z]
 
     by_plane.received()
@@ -406,6 +402,7 @@
     by_near.received()
     w_b[za] = summed(w_a, qb).astype(BF)
     by_far.start()
+    z_last.start()
     by_far.received()
     scale = 1.0 / (plan.nc * plan.dap)
     total = summed(w_b, qa)

time: 100 us -> 96.5 us (0.965)
  Pallas kernels: 98.7 us -> 95 us
    pallas_call x1, Pallas kernels: 96.4 us -> 92.7 us  [on_device(): pl.pallas_call(functools.partial(whole_kernel, plan), out_shape=(jax.Shap...]
where the time goes in v5:
time: 96.5 us; the launch traced here: 96.3 us
  Pallas kernels  95 us (98%)
  between operations  1.29 us (1%)
    pallas_call x1, Pallas kernels, on_device(): pl.pallas_call(functools.partial(whole_kernel, plan), out_shape=(jax.Shap...  92.7 us
    pallas_call x1, Pallas kernels, on_device(): pl.pallas_call(functools.partial(unpack_kernel, plan), out_shape=(jax.Sha...  2.32 us

profile of v5, /device:TPU:1, one launch (start us, length us, event | category | flops | bytes accessed | tf_op | source)
XLA Modules:
  0.0 96.3 jit_solution(14055313691930196597)
XLA Ops:
  1.3 92.7 %row_attention_gradients.1 = (bf16[256,256]{1,0:T(8,128)(2,1)}, f32[2,16,256]{2,1,0:T(8,128)}, bf16[2,16,80,128]{3,2,1,0:T(8,128)(2,1)}, f32[16,128]{1,0:T(8,128)}) custom-call(s32[1]{0:T(128)S(6)} %copy.12.ext_ref, bf16[64,4,256]{2,1,0:T(4,128)(2,1)} %bitcast.7, bf16[64,4,256]{2,1,0:T(4,128)(2,1)} %bitcast.8, bf16[8,4,256]{2,1,0:T(4,128)(2,1)} %bitcast.9, ...), custom_call_target="tpu_custom_call" | custom-call | tf_op jit(solution)/shard_map/row_attention_gradients/pallas_call | solution.py:463
  94.0 2.3 %unpack_gradients.1 = (bf16[64,4,256]{2,1,0:T(4,128)(2,1)}, f32[8,4,256]{2,1,0:T(4,128)}, f32[4,256,256]{2,1,0:T(8,128)}, f32[256,256]{1,0:T(8,128)}, f32[1,256]{1,0:T(1,128)}) custom-call(bf16[256,256]{1,0:T(8,128)(2,1)} %get-tuple-element.14.dr_ref, f32[2,16,256]{2,1,0:T(8,128)} %get-tuple-element.15.db_ref, ...), custom_call_target="tpu_custom_call" | custom-call | tf_op jit(solution)/shard_map/unpack_gradients/pallas_call | solution.py:514

commit v6 on v5

v6 whole, which is shorter than its diff:
```python
import functools
import math

import jax
import jax.numpy as jnp
from jax import lax
from jax.experimental import pallas as pl
from jax.experimental.pallas import tpu as pltpu
from jax.sharding import PartitionSpec as P

EPSILON = 1e-05
MASKED = -1000000000.0
LANES = 128
BF = jnp.bfloat16
F32 = jnp.float32
ANY = pl.BlockSpec(memory_space=pl.ANY)
VMEM = pl.BlockSpec(memory_space=pltpu.VMEM)
SMEM = pl.BlockSpec(memory_space=pltpu.SMEM)
LIMIT = 60 * 1024 * 1024


class Plan:
    def __init__(self, mesh, residues, channels, heads):
        self.nc = mesh.shape["crop"]
        self.nx = self.nc // 2
        dap = mesh.shape["dap"]
        self.ny = 4 if dap >= 16 else 2
        self.nz = dap // self.ny
        self.qb = 4 if self.nz >= 16 else 2
        self.qa = self.nz // self.qb
        self.dap = dap
        self.n = residues
        self.c = channels
        self.heads = heads
        self.own = residues // dap
        self.msg = self.ny * self.own
        self.blk = self.nz * self.own
        self.chunks = heads // self.ny
        self.tile = self.ny * self.nz * self.own
        self.cols = channels // self.ny
        self.flat = 10 * self.cols
        self.plane = self.nx * self.ny
        self.share = self.flat // (2 * self.nx)
        self.bits = 2 * self.chunks * self.own
        self.extra = 16


def nn(a, b):
    return lax.dot_general(a, b, (((1,), (0,)), ((), ())), preferred_element_type=F32)


def nt(a, b):
    return lax.dot_general(a, b, (((1,), (1,)), ((), ())), preferred_element_type=F32)


def tn(a, b):
    return lax.dot_general(a, b, (((0,), (0,)), ((), ())), preferred_element_type=F32)


def swap_matrix(plan, to_z):
    size = (plan.tile, plan.tile)
    row = lax.broadcasted_iota(jnp.int32, size, 0)
    col = lax.broadcasted_iota(jnp.int32, size, 1)
    za, az = (row, col) if to_z else (col, row)
    z, a, k = za // plan.msg, (za % plan.msg) // plan.own, za % plan.own
    return jnp.where(az == a * plan.blk + z * plan.own + k, 1.0, 0.0).astype(BF)


def place(plan):
    me = lax.axis_index("dap")
    return me // plan.nz, me % plan.nz


def signal(peer):
    pl.semaphore_signal(
        pltpu.get_barrier_semaphore(), inc=1, device_id=peer, device_id_type=pl.DeviceIdType.MESH
    )


def remote(src, dst, send, recv, peer):
    return pltpu.make_async_remote_copy(
        src_ref=src,
        dst_ref=dst,
        send_sem=send,
        recv_sem=recv,
        device_id=peer,
        device_id_type=pl.DeviceIdType.MESH,
    )


class Exchange:
    def __init__(self, make, count, like, sems):
        self.make, self.count, self.like, self.sems = make, count, like, sems

    def start(self, low=0, high=None):
        for i in range(low, self.count if high is None else high):
            src, dst, peer = self.make(i)
            remote(src, dst, self.sems.at[0], self.sems.at[1], peer).start()

    def received(self):
        pltpu.make_async_copy(self.like, self.like, self.sems.at[1]).wait()

    def sent(self):
        pltpu.make_async_copy(self.like, self.like, self.sems.at[0]).wait()


def keep(plan, start, count, put):
    at = start
    while at < start + count:
        s = at // plan.share
        end = min(start + count, (s + 1) * plan.share)
        low = s * plan.share
        put(slice(at - start, end - start), s, slice(at - low, end - low))
        at = end


def normalise(value):
    centred = value - jnp.mean(value, axis=-1, keepdims=True)
    inv_std = lax.rsqrt(jnp.mean(centred * centred, axis=-1, keepdims=True) + EPSILON)
    return centred * inv_std, inv_std


def summed(ref, count):
    out = ref[0].astype(F32)
    for i in range(1, count):
        out += ref[i].astype(F32)
    return out


def whole_kernel(
    plan, ext_ref, x_hbm, g_hbm, b_hbm, win_hbm, wout_hbm, gain_hbm,
    dr_out, db_out, w_all,
    x_in, g_in, b_in, win_ref, wout_ref, gain_ref,
    xg_s, xg_z, xg_ref, b_s, b_z, z_out, z_in, db_s, db_y,
    dn_s, dn_y, wg, w_cin, w_x, w_xin, w_a, w_b,
    lsem, xz, xy, by, bf, bn, z1, z2, dy, fy, wc, wx, wa, wb, gp, gc,
):
    y, z = place(plan)
    crop = lax.axis_index("crop")
    cx, core = crop // 2, crop % 2
    ny, nz, nx, blk, qa, qb = plan.ny, plan.nz, plan.nx, plan.blk, plan.qa, plan.qb
    za, zb = z // qb, z % qb
    n, ch, msg = plan.n, plan.c, plan.msg
    share, extra, plane = plan.share, plan.extra, plan.plane
    spot = cx * ny + y
    cols, chunks, heads = plan.cols, plan.chunks, plan.heads

    def zpeer(i):
        step = (i + 1) // 2
        zp = lax.rem(z + nz // 2 + step * (1 - 2 * (i % 2)), nz)
        return zp, {"dap": y * nz + zp}

    def ypeer(i):
        yp = lax.rem(y + i + 1, ny)
        return yp, {"dap": yp * nz + z}

    def ppeer(i):
        to = lax.rem(spot + i + 1, plane)
        return to, {"crop": (to // ny) * 2 + core, "dap": (to % ny) * nz + z}

    def apeer(i):
        return {"dap": y * nz + lax.rem(za + i + 1, qa) * qb + zb}

    def bpeer(i):
        return {"dap": y * nz + za * qb + lax.rem(zb + i + 1, qb)}

    def xpeer(i):
        xp = lax.rem(cx + i // ny + 1, nx)
        return {"crop": xp * 2 + core, "dap": (i % ny) * nz + z}

    def x_only(i):
        xp = lax.rem(cx + i + 1, nx)
        return xp, {"crop": xp * 2 + core}

    other = {"crop": cx * 2 + 1 - core}

    local = [
        pltpu.make_async_copy(s, d, lsem.at[i])
        for i, (s, d) in enumerate(
            [
                (b_hbm, b_in), (x_hbm, x_in), (g_hbm, g_in),
                (win_hbm, win_ref), (wout_hbm, wout_ref), (gain_hbm, gain_ref),
            ]
        )
    ]
    for c in local:
        c.start()
    for i in range(nz - 1):
        signal(zpeer(i)[1])
    for i in range(ny - 1):
        signal(ypeer(i)[1])
    for i in range(plane - ny):
        signal(xpeer(i))
    signal(other)
    for c in local[:3]:
        c.wait()
    xg_s[0] = x_in[...].reshape(nz, msg, ch)
    xg_s[1] = g_in[...].reshape(nz, msg, ch)
    lines = b_in[...].reshape(heads * plan.own, n)
    part = plan.chunks * plan.own
    for i in range(ny):
        for h in range(2):
            b_s[i, h * part : (h + 1) * part] = lines[
                i * part : (i + 1) * part, h * LANES : (h + 1) * LANES
            ]
    to_y = swap_matrix(plan, False)
    to_z = swap_matrix(plan, True)
    pl.semaphore_wait(pltpu.get_barrier_semaphore(), nz + plane - 1)

    def x_z(i):
        zp, peer = zpeer(i)
        return xg_s.at[:, zp], xg_z.at[:, z], peer

    def x_y(i):
        return xg_ref.at[:, mine], xg_ref.at[:, mine], ypeer(i)[1]

    def b_y(i):
        yp, peer = ypeer(i)
        return b_s.at[yp], b_z.at[za, zb, y], peer

    def b_far(i):
        return b_z.at[za, zb], b_z.at[za, zb], apeer(i)

    def b_near(i):
        return b_z.at[:, zb], b_z.at[:, zb], bpeer(i)

    mine = pl.ds(pl.multiple_of(y * blk, blk), blk)
    rows_z = Exchange(x_z, nz - 1, xg_z.at[:, pl.ds(0, nz - 1)], xz)
    rows_y = Exchange(x_y, ny - 1, xg_ref.at[:, pl.ds(0, (ny - 1) * blk)], xy)
    bias_y = Exchange(b_y, ny - 1, b_z.at[0, 0, pl.ds(0, ny - 1)], by)
    far = Exchange(b_far, qa - 1, b_z.at[pl.ds(0, qa - 1), 0], bf)
    near = Exchange(b_near, qb - 1, b_z.at[:, pl.ds(0, qb - 1)], bn)

    bias_y.start()
    rows_z.start()
    b_z[za, zb, y] = b_s[y]
    xg_z[:, z] = xg_s[:, z]
    for c in local[3:]:
        c.wait()
    source = lax.broadcasted_iota(jnp.int32, (ch, 4 * cols), 0) - y * cols
    target = lax.broadcasted_iota(jnp.int32, (ch, 4 * cols), 1)
    w_own = jnp.zeros((ch, 4 * cols), F32)
    for p in range(4):
        pick = jnp.logical_and(source == target - p * cols, target // cols == p)
        w_own += nn(win_ref[p], jnp.where(pick, 1.0, 0.0).astype(BF))
    w_own = w_own.astype(BF)
    w_last = wout_ref[pl.ds(pl.multiple_of(y * cols, cols), cols)]
    bias_y.received()
    far.start()
    rows_z.received()
    for t in range(2):
        rows = nn(to_y, xg_z[t].reshape(plan.tile, ch)).astype(BF)
        xg_ref[pl.ds(t * ny, ny), mine] = rows.reshape(ny, blk, ch)
    far.received()
    near.start()
    rows_y.start()
    near.received()
    pieces = b_z[...].reshape(plan.dap * plan.bits, LANES)
    size = (n, plan.dap * plan.bits)
    line = lax.broadcasted_iota(jnp.int32, size, 0)
    first = (line % blk) // plan.own * (ny * plan.bits) + line // blk * plan.bits
    off = lax.broadcasted_iota(jnp.int32, size, 1) - first - line % plan.own
    bias = []
    for h in range(chunks):
        sides = []
        for side in range(2):
            pick = jnp.where(off == (side * chunks + h) * plan.own, 1.0, 0.0).astype(BF)
            sides.append(nn(pick, pieces))
        bias.append(jnp.concatenate(sides, axis=1))
    rows_y.received()

    size = ch // heads
    mult = 1.0 / math.sqrt(size)
    extent = ext_ref[0]
    gain = gain_ref[...]
    row_valid = lax.broadcasted_iota(jnp.int32, (n, ch), 0) < extent
    normal, normed, mg, projected, d_gated = [], [], [], [], []
    for j in range(ny):
        normal.append(normalise(xg_ref[j].astype(F32))[0])
        normed.append((normal[j] * gain).astype(BF))
        projected.append(nn(normed[j], w_own))
        mg.append(jnp.where(row_valid, xg_ref[ny + j].astype(F32), 0.0).astype(BF))
        d_gated.append(nt(mg[j], w_last))

    def across(parts, p):
        return jnp.concatenate([a[:, p * cols : (p + 1) * cols] for a in parts], axis=1)

    q, k, v, gl = [across(projected, p).astype(BF) for p in range(4)]
    gate = jax.nn.sigmoid(gl.astype(F32))
    d_gated = across(d_gated, 0)
    da = (d_gated * gate).astype(BF)
    col_valid = lax.broadcasted_iota(jnp.int32, (n, n), 1) < extent
    group_of = lax.broadcasted_iota(jnp.int32, (1, ch), 1) // size
    att = dv = dq = dk = jnp.zeros((n, ch), F32)
    d_bias = [jnp.zeros((n, n), F32)] * chunks

    def first_z(i):
        zp, peer = zpeer(i)
        part = pl.ds(0, chunks)
        return z_out.at[zp, part], z_in.at[z, part], peer

    def last_z(i):
        zp, peer = zpeer(i)
        return z_out.at[zp, chunks], z_in.at[z, chunks], peer

    others = pl.ds(0, nz - 1)
    z_first = Exchange(first_z, nz - 1, z_in.at[others, pl.ds(0, chunks)], z1)
    z_last = Exchange(last_z, nz - 1, z_in.at[others, chunks], z2)

    for h in range(chunks):
        for j in range(ny):
            own = jnp.where(group_of == j * chunks + h, 1.0, 0.0).astype(BF)
            qh, kh, vh, dah = q * own, k * own, v * own, da * own
            scores = nt(qh, k) * mult + bias[h]
            scores = jnp.where(col_valid, scores, MASKED)
            expo = jnp.exp(scores - jnp.max(scores, axis=-1, keepdims=True))
            probs = expo * (1.0 / jnp.sum(expo, axis=-1, keepdims=True))
            pb = probs.astype(BF)
            d_probs = nt(dah, v)
            total = jnp.sum(probs * d_probs, axis=-1, keepdims=True)
            d_scores = probs * (d_probs - total)
            dsb = d_scores.astype(BF)
            d_bias[h] += d_scores
            att += nn(pb, vh)
            dv += tn(pb, dah)
            dq += nn(dsb, kh)
            dk += tn(dsb, qh)
        z_out[:, h] = nn(to_z, d_bias[h].astype(BF)).astype(BF).reshape(nz, msg, n)
    z_first.start()
    gated = (att * gate).astype(BF)
    grads = [dq * mult, dk * mult, dv, d_gated * att * gate * (1.0 - gate)]
    packed = [across(grads, j).astype(BF) for j in range(ny)]
    d_in = jnp.zeros((ch, 4 * cols), F32)
    d_last = jnp.zeros((cols, ch), F32)
    d_gain = jnp.zeros((1, ch), F32)
    for j in range(ny):
        d_in += tn(normed[j], packed[j])
        d_last += tn(gated[:, j * cols : (j + 1) * cols], mg[j])
        d_normed = nt(packed[j], w_own)
        d_gain += jnp.sum(d_normed * normal[j], axis=0, keepdims=True)
        dn_s[j] = d_normed.astype(BF).reshape(ny, blk, ch)

    at = 0
    for term, lanes in ((d_in, 4 * cols), (d_last, ch)):
        term = term.astype(BF)
        for side in range(lanes // LANES):
            piece = term[:, side * LANES : (side + 1) * LANES]

            def put(rows, s, to, piece=piece):
                wg[s // nx, s % nx, to] = piece[rows]

            keep(plan, at, piece.shape[0], put)
            at += piece.shape[0]
    line = lax.broadcasted_iota(jnp.int32, (extra, LANES), 0)
    lo = jnp.broadcast_to(d_gain[:, :LANES], (extra, LANES))
    hi = jnp.broadcast_to(d_gain[:, LANES:], (extra, LANES))
    block = jnp.where(line == 0, lo, jnp.where(line == 1, hi, 0.0)).astype(BF)
    for core_of in range(2):
        wg[core_of, :, share:] = jnp.broadcast_to(block[None], (nx, extra, LANES))

    def w_c(i):
        return wg.at[1 - core], w_cin, other

    def w_across(i):
        to, peer = x_only(i)
        return w_x.at[to], w_xin.at[cx], peer

    def w_near(i):
        return w_a.at[zb], w_a.at[zb], bpeer(i)

    def w_far(i):
        return w_b.at[za], w_b.at[za], apeer(i)

    def g_plane(i):
        part = w_all.at[core, spot]
        return part, part, ppeer(i)[1]

    def g_core(i):
        return w_all.at[core], w_all.at[core], other

    by_core = Exchange(w_c, 1, w_cin, wc)
    by_x = Exchange(w_across, nx - 1, w_xin.at[pl.ds(0, nx - 1)], wx)
    by_near = Exchange(w_near, qb - 1, w_a.at[pl.ds(0, qb - 1)], wa)
    by_far = Exchange(w_far, qa - 1, w_b.at[pl.ds(0, qa - 1)], wb)
    to_plane = Exchange(g_plane, plane - 1, w_all.at[0, pl.ds(0, plane - 1)], gp)
    to_core = Exchange(g_core, 1, w_all.at[0], gc)

    def dn_y_(i):
        yp, peer = ypeer(i)
        return dn_s.at[:, yp], dn_y.at[i], peer

    def db_y_(i):
        yp, peer = ypeer(i)
        return db_s.at[yp], db_y.at[y], peer

    dn_by_y = Exchange(dn_y_, ny - 1, dn_y, dy)
    db_by_y = Exchange(db_y_, ny - 1, db_y.at[pl.ds(0, ny - 1)], fy)

    by_core.start()
    dn_by_y.start()
    by_core.received()
    w_x[...] = (wg[core].astype(F32) + w_cin[...].astype(F32)).astype(BF)
    by_x.start()
    w_xin[cx] = w_x[cx]
    by_x.received()
    w_a[zb] = summed(w_xin, nx).astype(BF)
    by_near.start()

    dn_by_y.received()
    total = dn_s[:, y].astype(F32)
    for i in range(ny - 1):
        total += dn_y[i].astype(F32)
    total = total.reshape(plan.tile, ch)
    own_x, inv_std = normalise(xg_ref[pl.ds(0, ny), mine].astype(F32).reshape(plan.tile, ch))
    scaled = total * gain
    d_row = inv_std * (
        scaled
        - jnp.mean(scaled, axis=-1, keepdims=True)
        - own_x * jnp.mean(scaled * own_x, axis=-1, keepdims=True)
    )
    z_out[:, chunks] = nn(to_z, d_row.astype(BF)).astype(BF).reshape(nz, msg, ch)

    by_near.received()
    w_b[za] = summed(w_a, qb).astype(BF)
    by_far.start()
    z_last.start()
    z_in[z] = z_out[z]
    z_first.received()
    total = z_in[0, pl.ds(0, chunks)].astype(F32)
    for i in range(1, nz):
        total += z_in[i, pl.ds(0, chunks)].astype(F32)
    for i in range(ny):
        for h in range(chunks):
            to = slice(h * plan.own, (h + 1) * plan.own)
            db_s[i, to] = total[h, i * plan.own : (i + 1) * plan.own]
    db_by_y.start()
    db_y[y] = db_s[y]
    by_far.received()
    w_all[core, spot] = summed(w_b, qa).astype(BF)
    to_plane.start()
    db_by_y.received()
    db_out[...] = db_y[...]
    z_last.received()
    dr_out[...] = z_in[:, chunks].reshape(n, ch)
    to_plane.received()
    to_core.start()

    exchanges = [rows_z, rows_y, bias_y, far, near, by_core, by_x, by_near, by_far]
    for e in exchanges + [to_plane, dn_by_y, db_by_y, z_first, z_last]:
        e.sent()
    to_core.received()
    to_core.sent()


def unpack_kernel(plan, dr_ref, db_ref, w_all, dr_out, db_out, win_out, wout_out, gain_out):
    scale = 1.0 / (plan.nc * plan.dap)
    ch, cols, nx, ny, share = plan.c, plan.cols, plan.nx, plan.ny, plan.share
    dr_out[...] = dr_ref[...].reshape(dr_out.shape)
    db_out[...] = db_ref[...].reshape(db_out.shape)
    total = w_all[0, 0, share:].astype(F32)
    for y in range(1, ny):
        total += w_all[0, y, share:].astype(F32)
    gain_out[:, :LANES] = total[0:1] * scale
    gain_out[:, LANES:] = total[1:2] * scale

    def part(y, start, count):
        found = []

        def take(rows, s, at):
            found.append(w_all[s // nx, s % nx * ny + y, at].astype(F32) * scale)

        keep(plan, start, count, take)
        return jnp.concatenate(found, axis=0)

    sides = 4 * cols // LANES
    full = [
        jnp.concatenate([part(y, side * ch, ch) for side in range(sides)], axis=1)
        for y in range(ny)
    ]
    for p in range(4):
        own = slice(p * cols, (p + 1) * cols)
        win_out[p] = jnp.concatenate([a[:, own] for a in full], axis=1)
    for y in range(ny):
        low = [part(y, sides * ch + side * cols, cols) for side in range(2)]
        wout_out[y * cols : (y + 1) * cols] = jnp.concatenate(low, axis=1)


def dma(*shape):
    return pltpu.SemaphoreType.DMA(shape)


def on_device(plan, x, upstream, bias, extents, w_in, w_final, gain):
    ny, nz, n, ch = plan.ny, plan.nz, plan.n, plan.c
    msg, blk, chunks, heads = plan.msg, plan.blk, plan.chunks, plan.heads
    total, plane = plan.share + plan.extra, plan.plane

    def buf(*shape, kind=BF):
        return pltpu.VMEM(shape, kind)

    sums = pl.pallas_call(
        functools.partial(whole_kernel, plan),
        out_shape=(
            jax.ShapeDtypeStruct((n, ch), BF),
            jax.ShapeDtypeStruct((ny, chunks * plan.own, n), F32),
            jax.ShapeDtypeStruct((2, plane, total, LANES), BF),
        ),
        in_specs=[SMEM] + [ANY] * 6,
        out_specs=(VMEM,) * 3,
        scratch_shapes=[
            buf(plan.dap, plan.own, ch),
            buf(plan.dap, plan.own, ch),
            buf(heads, plan.own, n),
            buf(4, ch, ch),
            buf(ch, ch),
            buf(1, ch, kind=F32),
            buf(2, nz, msg, ch),
            buf(2, nz, msg, ch),
            buf(2 * ny, n, ch),
            buf(ny, plan.bits, LANES),
            buf(plan.qa, plan.qb, ny, plan.bits, LANES),
            buf(nz, chunks + 1, msg, n),
            buf(nz, chunks + 1, msg, n),
            buf(ny, chunks * plan.own, n, kind=F32),
            buf(ny, chunks * plan.own, n, kind=F32),
            buf(ny, ny, blk, ch),
            buf(ny - 1, ny, blk, ch),
            buf(2, plan.nx, total, LANES),
            buf(plan.nx, total, LANES),
            buf(plan.nx, total, LANES),
            buf(plan.nx, total, LANES),
            buf(plan.qb, total, LANES),
            buf(plan.qa, total, LANES),
            dma(6),
            *[dma(2)] * 15,
        ],
        compiler_params=pltpu.CompilerParams(
            collective_id=0, has_side_effects=True, vmem_limit_bytes=LIMIT
        ),
        name="row_attention_gradients",
    )(
        extents, x[0], upstream[0], bias[0], w_in, w_final, gain.reshape(1, ch)
    )
    d_rows, d_bias, d_in, d_out, d_gain = pl.pallas_call(
        functools.partial(unpack_kernel, plan),
        out_shape=(
            jax.ShapeDtypeStruct((plan.dap, plan.own, ch), BF),
            jax.ShapeDtypeStruct((heads, plan.own, n), F32),
            jax.ShapeDtypeStruct((4, ch, ch), F32),
            jax.ShapeDtypeStruct((ch, ch), F32),
            jax.ShapeDtypeStruct((1, ch), F32),
        ),
        in_specs=[VMEM] * 3,
        out_specs=(VMEM,) * 5,
        compiler_params=pltpu.CompilerParams(vmem_limit_bytes=LIMIT),
        name="unpack_gradients",
    )(*sums)
    return (d_rows[None], d_bias[None], d_in, d_out, d_gain.reshape(ch))


def solution(mesh):
    split = P("crop", None, "dap", None)

    def whole(*arrays):
        plan = Plan(mesh, arrays[0].shape[2], arrays[0].shape[3], arrays[2].shape[1])
        return jax.shard_map(
            functools.partial(on_device, plan),
            mesh=mesh,
            in_specs=(split, split, split, P("crop"), P(), P(), P()),
            out_specs=(split, split, P(), P(), P()),
            check_vma=False,
        )(*arrays)

    return whole
```

time: 96.5 us -> 91.7 us (0.950)
  Pallas kernels: 95 us -> 90.2 us
    pallas_call x1, Pallas kernels: 92.7 us -> 87.6 us  [on_device(): pl.pallas_call(functools.partial(whole_kernel, plan), out_shape=(jax.Shap...]
where the time goes in v6:
time: 91.7 us; the launch traced here: 91.5 us
  Pallas kernels  90.2 us (98%)
  between operations  1.29 us (1%)
    pallas_call x1, Pallas kernels, on_device(): pl.pallas_call(functools.partial(whole_kernel, plan), out_shape=(jax.Shap...  87.6 us
    pallas_call x1, Pallas kernels, on_device(): pl.pallas_call(functools.partial(unpack_kernel, plan), out_shape=(jax.Sha...  2.63 us

profile of v6, /device:TPU:1, one launch (start us, length us, event | category | flops | bytes accessed | tf_op | source)
XLA Modules:
  0.0 91.5 jit_solution(11891892953046444273)
XLA Ops:
  1.3 87.6 %row_attention_gradients.1 = (bf16[256,256]{1,0:T(8,128)(2,1)}, f32[4,8,256]{2,1,0:T(8,128)}, bf16[2,16,96,128]{3,2,1,0:T(8,128)(2,1)}) custom-call(s32[1]{0:T(128)S(6)} %copy.12.ext_ref, bf16[64,4,256]{2,1,0:T(4,128)(2,1)} %bitcast.7, bf16[64,4,256]{2,1,0:T(4,128)(2,1)} %bitcast.8, bf16[8,4,256]{2,1,0:T(4,128)(2,1)} %bitcast.9, ...), custom_call_target="tpu_custom_call" | custom-call | tf_op jit(solution)/shard_map/row_attention_gradients/pallas_call | solution.py:500
  88.9 2.6 %unpack_gradients.1 = (bf16[64,4,256]{2,1,0:T(4,128)(2,1)}, f32[8,4,256]{2,1,0:T(4,128)}, f32[4,256,256]{2,1,0:T(8,128)}, f32[256,256]{1,0:T(8,128)}, f32[1,256]{1,0:T(1,128)}) custom-call(bf16[256,256]{1,0:T(8,128)(2,1)} %get-tuple-element.13.dr_ref, f32[4,8,256]{2,1,0:T(8,128)} %get-tuple-element.14.db_ref, bf16[2,16,96,128]{3,2,1,0:T(8,128)(2,1)} %get-tuple-element.15.w_all), custom_call_target="tpu_custom_call" | custom-call | tf_op jit(solution)/shard_map/unpack_gradients/pallas_call | solution.py:543

commit v7 on v6

--- a/solution.py
+++ b/solution.py
@@ -207,12 +207,20 @@
     to_z = swap_matrix(plan, True)
     pl.semaphore_wait(pltpu.get_barrier_semaphore(), nz + plane - 1)
 
-    def x_z(i):
-        zp, peer = zpeer(i)
-        return xg_s.at[:, zp], xg_z.at[:, z], peer
-
-    def x_y(i):
-        return xg_ref.at[:, mine], xg_ref.at[:, mine], ypeer(i)[1]
+    def over_z(t):
+        def x_z(i):
+            zp, peer = zpeer(i)
+            return xg_s.at[t, zp], xg_z.at[t, z], peer
+
+        return Exchange(x_z, nz - 1, xg_z.at[t, pl.ds(0, nz - 1)], xz.at[t])
+
+    def over_y(t):
+        def x_y(i):
+            part = xg_ref.at[pl.ds(t * ny, ny), mine]
+            return part, part, ypeer(i)[1]
+
+        like = xg_ref.at[pl.ds(t * ny, ny), pl.ds(0, (ny - 1) * blk)]
+        return Exchange(x_y, ny - 1, like, xy.at[t])
 
     def b_y(i):
         yp, peer = ypeer(i)
@@ -225,14 +233,14 @@
         return b_z.at[:, zb], b_z.at[:, zb], bpeer(i)
 
     mine = pl.ds(pl.multiple_of(y * blk, blk), blk)
-    rows_z = Exchange(x_z, nz - 1, xg_z.at[:, pl.ds(0, nz - 1)], xz)
-    rows_y = Exchange(x_y, ny - 1, xg_ref.at[:, pl.ds(0, (ny - 1) * blk)], xy)
+    rows_z, rows_y = [over_z(t) for t in range(2)], [over_y(t) for t in range(2)]
     bias_y = Exchange(b_y, ny - 1, b_z.at[0, 0, pl.ds(0, ny - 1)], by)
     far = Exchange(b_far, qa - 1, b_z.at[pl.ds(0, qa - 1), 0], bf)
     near = Exchange(b_near, qb - 1, b_z.at[:, pl.ds(0, qb - 1)], bn)
 
     bias_y.start()
-    rows_z.start()
+    rows_z[0].start()
+    rows_z[1].start()
     b_z[za, zb, y] = b_s[y]
     xg_z[:, z] = xg_s[:, z]
     for c in local[3:]:
@@ -247,13 +255,18 @@
     w_last = wout_ref[pl.ds(pl.multiple_of(y * cols, cols), cols)]
     bias_y.received()
     far.start()
-    rows_z.received()
-    for t in range(2):
+
+    def regroup(t):
+        rows_z[t].received()
         rows = nn(to_y, xg_z[t].reshape(plan.tile, ch)).astype(BF)
         xg_ref[pl.ds(t * ny, ny), mine] = rows.reshape(ny, blk, ch)
+
+    regroup(0)
     far.received()
     near.start()
-    rows_y.start()
+    rows_y[0].start()
+    regroup(1)
+    rows_y[1].start()
     near.received()
     pieces = b_z[...].reshape(plan.dap * plan.bits, LANES)
     size = (n, plan.dap * plan.bits)
@@ -267,7 +280,7 @@
             pick = jnp.where(off == (side * chunks + h) * plan.own, 1.0, 0.0).astype(BF)
             sides.append(nn(pick, pieces))
         bias.append(jnp.concatenate(sides, axis=1))
-    rows_y.received()
+    rows_y[0].received()
 
     size = ch // heads
     mult = 1.0 / math.sqrt(size)
@@ -279,6 +292,8 @@
         normal.append(normalise(xg_ref[j].astype(F32))[0])
         normed.append((normal[j] * gain).astype(BF))
         projected.append(nn(normed[j], w_own))
+    rows_y[1].received()
+    for j in range(ny):
         mg.append(jnp.where(row_valid, xg_ref[ny + j].astype(F32), 0.0).astype(BF))
         d_gated.append(nt(mg[j], w_last))
 
@@ -445,7 +460,7 @@
     to_plane.received()
     to_core.start()
 
-    exchanges = [rows_z, rows_y, bias_y, far, near, by_core, by_x, by_near, by_far]
+    exchanges = [*rows_z, *rows_y, bias_y, far, near, by_core, by_x, by_near, by_far]
     for e in exchanges + [to_plane, dn_by_y, db_by_y, z_first, z_last]:
         e.sent()
     to_core.received()
@@ -531,7 +546,9 @@
             buf(plan.qb, total, LANES),
             buf(plan.qa, total, LANES),
             dma(6),
-            *[dma(2)] * 15,
+            dma(2, 2),
+            dma(2, 2),
+            *[dma(2)] * 13,
         ],
         compiler_params=pltpu.CompilerParams(
             collective_id=0, has_side_effects=True, vmem_limit_bytes=LIMIT

time: 91.7 us -> 89 us (0.971)
  Pallas kernels: 90.2 us -> 87.6 us
    pallas_call x1, Pallas kernels: 87.6 us -> 84.9 us  [on_device(): pl.pallas_call(functools.partial(whole_kernel, plan), out_shape=(jax.Shap...]
where the time goes in v7:
time: 89 us; the launch traced here: 88.8 us
  Pallas kernels  87.6 us (98%)
  between operations  1.29 us (1%)
    pallas_call x1, Pallas kernels, on_device(): pl.pallas_call(functools.partial(whole_kernel, plan), out_shape=(jax.Shap...  84.9 us
    pallas_call x1, Pallas kernels, on_device(): pl.pallas_call(functools.partial(unpack_kernel, plan), out_shape=(jax.Sha...  2.63 us

profile of v7, /device:TPU:1, one launch (start us, length us, event | category | flops | bytes accessed | tf_op | source)
XLA Modules:
  0.0 88.8 jit_solution(9651470528045231997)
XLA Ops:
  1.3 84.9 %row_attention_gradients.1 = (bf16[256,256]{1,0:T(8,128)(2,1)}, f32[4,8,256]{2,1,0:T(8,128)}, bf16[2,16,96,128]{3,2,1,0:T(8,128)(2,1)}) custom-call(s32[1]{0:T(128)S(6)} %copy.12.ext_ref, bf16[64,4,256]{2,1,0:T(4,128)(2,1)} %bitcast.7, bf16[64,4,256]{2,1,0:T(4,128)(2,1)} %bitcast.8, bf16[8,4,256]{2,1,0:T(4,128)(2,1)} %bitcast.9, ...), custom_call_target="tpu_custom_call" | custom-call | tf_op jit(solution)/shard_map/row_attention_gradients/pallas_call | solution.py:515
  86.2 2.6 %unpack_gradients.1 = (bf16[64,4,256]{2,1,0:T(4,128)(2,1)}, f32[8,4,256]{2,1,0:T(4,128)}, f32[4,256,256]{2,1,0:T(8,128)}, f32[256,256]{1,0:T(8,128)}, f32[1,256]{1,0:T(1,128)}) custom-call(bf16[256,256]{1,0:T(8,128)(2,1)} %get-tuple-element.13.dr_ref, f32[4,8,256]{2,1,0:T(8,128)} %get-tuple-element.14.db_ref, bf16[2,16,96,128]{3,2,1,0:T(8,128)(2,1)} %get-tuple-element.15.w_all), custom_call_target="tpu_custom_call" | custom-call | tf_op jit(solution)/shard_map/unpack_gradients/pallas_call | solution.py:560

commit v8 on v7

--- a/solution.py
+++ b/solution.py
@@ -132,8 +132,8 @@
     dr_out, db_out, w_all,
     x_in, g_in, b_in, win_ref, wout_ref, gain_ref,
     xg_s, xg_z, xg_ref, b_s, b_z, z_out, z_in, db_s, db_y,
-    dn_s, dn_y, wg, w_cin, w_x, w_xin, w_a, w_b,
-    lsem, xz, xy, by, bf, bn, z1, z2, dy, fy, wc, wx, wa, wb, gp, gc,
+    dn_s, dn_y, wg, w_in, w_a, w_b,
+    lsem, xz, xy, by, bf, bn, z1, z2, dy, fy, wc, wa, wb, gp, gc,
 ):
     y, z = place(plan)
     crop = lax.axis_index("crop")
@@ -168,9 +168,9 @@
         xp = lax.rem(cx + i // ny + 1, nx)
         return {"crop": xp * 2 + core, "dap": (i % ny) * nz + z}
 
-    def x_only(i):
-        xp = lax.rem(cx + i + 1, nx)
-        return xp, {"crop": xp * 2 + core}
+    def cpeer(i):
+        to = lax.rem(crop + i + 1, plan.nc)
+        return to, {"crop": to}
 
     other = {"crop": cx * 2 + 1 - core}
 
@@ -192,6 +192,8 @@
     for i in range(plane - ny):
         signal(xpeer(i))
     signal(other)
+    for i in range(nx - 1):
+        signal({"crop": lax.rem(cx + i + 1, nx) * 2 + 1 - core})
     for c in local[:3]:
         c.wait()
     xg_s[0] = x_in[...].reshape(nz, msg, ch)
@@ -205,7 +207,7 @@
             ]
     to_y = swap_matrix(plan, False)
     to_z = swap_matrix(plan, True)
-    pl.semaphore_wait(pltpu.get_barrier_semaphore(), nz + plane - 1)
+    pl.semaphore_wait(pltpu.get_barrier_semaphore(), nz + plane + nx - 2)
 
     def over_z(t):
         def x_z(i):
@@ -373,12 +375,9 @@
     for core_of in range(2):
         wg[core_of, :, share:] = jnp.broadcast_to(block[None], (nx, extra, LANES))
 
-    def w_c(i):
-        return wg.at[1 - core], w_cin, other
-
-    def w_across(i):
-        to, peer = x_only(i)
-        return w_x.at[to], w_xin.at[cx], peer
+    def w_crop(i):
+        to, peer = cpeer(i)
+        return wg.at[to % 2, to // 2], w_in.at[crop], peer
 
     def w_near(i):
         return w_a.at[zb], w_a.at[zb], bpeer(i)
@@ -393,8 +392,7 @@
     def g_core(i):
         return w_all.at[core], w_all.at[core], other
 
-    by_core = Exchange(w_c, 1, w_cin, wc)
-    by_x = Exchange(w_across, nx - 1, w_xin.at[pl.ds(0, nx - 1)], wx)
+    by_crop = Exchange(w_crop, plan.nc - 1, w_in.at[pl.ds(0, plan.nc - 1)], wc)
     by_near = Exchange(w_near, qb - 1, w_a.at[pl.ds(0, qb - 1)], wa)
     by_far = Exchange(w_far, qa - 1, w_b.at[pl.ds(0, qa - 1)], wb)
     to_plane = Exchange(g_plane, plane - 1, w_all.at[0, pl.ds(0, plane - 1)], gp)
@@ -411,14 +409,11 @@
     dn_by_y = Exchange(dn_y_, ny - 1, dn_y, dy)
     db_by_y = Exchange(db_y_, ny - 1, db_y.at[pl.ds(0, ny - 1)], fy)
 
-    by_core.start()
+    by_crop.start()
     dn_by_y.start()
-    by_core.received()
-    w_x[...] = (wg[core].astype(F32) + w_cin[...].astype(F32)).astype(BF)
-    by_x.start()
-    w_xin[cx] = w_x[cx]
-    by_x.received()
-    w_a[zb] = summed(w_xin, nx).astype(BF)
+    w_in[crop] = wg[core, cx]
+    by_crop.received()
+    w_a[zb] = summed(w_in, plan.nc).astype(BF)
     by_near.start()
 
     dn_by_y.received()
@@ -460,7 +455,7 @@
     to_plane.received()
     to_core.start()
 
-    exchanges = [*rows_z, *rows_y, bias_y, far, near, by_core, by_x, by_near, by_far]
+    exchanges = [*rows_z, *rows_y, bias_y, far, near, by_crop, by_near, by_far]
     for e in exchanges + [to_plane, dn_by_y, db_by_y, z_first, z_last]:
         e.sent()
     to_core.received()
@@ -540,15 +535,13 @@
             buf(ny, ny, blk, ch),
             buf(ny - 1, ny, blk, ch),
             buf(2, plan.nx, total, LANES),
-            buf(plan.nx, total, LANES),
-            buf(plan.nx, total, LANES),
-            buf(plan.nx, total, LANES),
+            buf(plan.nc, total, LANES),
             buf(plan.qb, total, LANES),
             buf(plan.qa, total, LANES),
             dma(6),
             dma(2, 2),
             dma(2, 2),
-            *[dma(2)] * 13,
+            *[dma(2)] * 12,
         ],
         compiler_params=pltpu.CompilerParams(
             collective_id=0, has_side_effects=True, vmem_limit_bytes=LIMIT

time: 89 us -> 89 us (level)
  no operation moved by 1% of the time
where the time goes in v8:
time: 89 us; the launch traced here: 88.9 us
  Pallas kernels  87.6 us (98%)
  between operations  1.29 us (1%)
    pallas_call x1, Pallas kernels, on_device(): pl.pallas_call(functools.partial(whole_kernel, plan), out_shape=(jax.Shap...  84.9 us
    pallas_call x1, Pallas kernels, on_device(): pl.pallas_call(functools.partial(unpack_kernel, plan), out_shape=(jax.Sha...  2.63 us

profile of v8, /device:TPU:1, one launch (start us, length us, event | category | flops | bytes accessed | tf_op | source)
XLA Modules:
  0.0 88.9 jit_solution(537077645380066489)
XLA Ops:
  1.3 84.9 %row_attention_gradients.1 = (bf16[256,256]{1,0:T(8,128)(2,1)}, f32[4,8,256]{2,1,0:T(8,128)}, bf16[2,16,96,128]{3,2,1,0:T(8,128)(2,1)}) custom-call(s32[1]{0:T(128)S(6)} %copy.12.ext_ref, bf16[64,4,256]{2,1,0:T(4,128)(2,1)} %bitcast.7, bf16[64,4,256]{2,1,0:T(4,128)(2,1)} %bitcast.8, bf16[8,4,256]{2,1,0:T(4,128)(2,1)} %bitcast.9, ...), custom_call_target="tpu_custom_call" | custom-call | tf_op jit(solution)/shard_map/row_attention_gradients/pallas_call | solution.py:510
  86.2 2.6 %unpack_gradients.1 = (bf16[64,4,256]{2,1,0:T(4,128)(2,1)}, f32[8,4,256]{2,1,0:T(4,128)}, f32[4,256,256]{2,1,0:T(8,128)}, f32[256,256]{1,0:T(8,128)}, f32[1,256]{1,0:T(1,128)}) custom-call(bf16[256,256]{1,0:T(8,128)(2,1)} %get-tuple-element.13.dr_ref, f32[4,8,256]{2,1,0:T(8,128)} %get-tuple-element.14.db_ref, bf16[2,16,96,128]{3,2,1,0:T(8,128)(2,1)} %get-tuple-element.15.w_all), custom_call_target="tpu_custom_call" | custom-call | tf_op jit(solution)/shard_map/unpack_gradients/pallas_call | solution.py:553

commit v9 on v8

--- a/solution.py
+++ b/solution.py
@@ -448,12 +448,12 @@
     by_far.received()
     w_all[core, spot] = summed(w_b, qa).astype(BF)
     to_plane.start()
+    to_plane.received()
+    to_core.start()
     db_by_y.received()
     db_out[...] = db_y[...]
     z_last.received()
     dr_out[...] = z_in[:, chunks].reshape(n, ch)
-    to_plane.received()
-    to_core.start()
 
     exchanges = [*rows_z, *rows_y, bias_y, far, near, by_crop, by_near, by_far]
     for e in exchanges + [to_plane, dn_by_y, db_by_y, z_first, z_last]:

time: 89 us -> 89 us (level)
  no operation moved by 1% of the time
where the time goes in v9:
time: 89 us; the launch traced here: 88.9 us
  Pallas kernels  87.6 us (98%)
  between operations  1.29 us (1%)
    pallas_call x1, Pallas kernels, on_device(): pl.pallas_call(functools.partial(whole_kernel, plan), out_shape=(jax.Shap...  84.9 us
    pallas_call x1, Pallas kernels, on_device(): pl.pallas_call(functools.partial(unpack_kernel, plan), out_shape=(jax.Sha...  2.63 us

profile of v9, /device:TPU:1, one launch (start us, length us, event | category | flops | bytes accessed | tf_op | source)
XLA Modules:
  0.0 88.9 jit_solution(8912080980053373367)
XLA Ops:
  1.3 84.9 %row_attention_gradients.1 = (bf16[256,256]{1,0:T(8,128)(2,1)}, f32[4,8,256]{2,1,0:T(8,128)}, bf16[2,16,96,128]{3,2,1,0:T(8,128)(2,1)}) custom-call(s32[1]{0:T(128)S(6)} %copy.12.ext_ref, bf16[64,4,256]{2,1,0:T(4,128)(2,1)} %bitcast.7, bf16[64,4,256]{2,1,0:T(4,128)(2,1)} %bitcast.8, bf16[8,4,256]{2,1,0:T(4,128)(2,1)} %bitcast.9, ...), custom_call_target="tpu_custom_call" | custom-call | tf_op jit(solution)/shard_map/row_attention_gradients/pallas_call | solution.py:510
  86.2 2.6 %unpack_gradients.1 = (bf16[64,4,256]{2,1,0:T(4,128)(2,1)}, f32[8,4,256]{2,1,0:T(4,128)}, f32[4,256,256]{2,1,0:T(8,128)}, f32[256,256]{1,0:T(8,128)}, f32[1,256]{1,0:T(1,128)}) custom-call(bf16[256,256]{1,0:T(8,128)(2,1)} %get-tuple-element.13.dr_ref, f32[4,8,256]{2,1,0:T(8,128)} %get-tuple-element.14.db_ref, bf16[2,16,96,128]{3,2,1,0:T(8,128)(2,1)} %get-tuple-element.15.w_all), custom_call_target="tpu_custom_call" | custom-call | tf_op jit(solution)/shard_map/unpack_gradients/pallas_call | solution.py:553
